TPU v7x, 128 devices: a whole 4x4x4 slice. The times are simulated.
128 devices in a mesh: ctx: 16 (over z_lo, y, core), head: 8 (over x, z_hi).
Axes of the slice: x: 4, y: 4, z: 4 (z_hi: 2, z_lo: 2; z = z_hi * 2 + z_lo), core: 2. Of those that a mesh axis runs over, the one named last changes fastest.
Arguments:
- main_queries: bfloat16 [4096, 128, 576], P('ctx', 'head'), may hold values from -6 to 6
- latents: bfloat16 [4096, 576], P('ctx'), may hold values from -6 to 6
- saved_lse: float32 [4096, 128], P('ctx', 'head'), may hold values from 9 to 12
- index_queries: bfloat16 [4096, 64, 128], P('ctx', 'head'), may hold values from -7 to 7, as said below
- index_keys: bfloat16 [4096, 128], P('ctx'), may hold values from -7 to 7, as said below
- head_weights: bfloat16 [4096, 64], P('ctx', 'head'), may hold values from 0.019897461 to 0.25
- row_weight: float32 [4096], P('ctx'), may hold values from 4096 to 16384
- block_offsets: int32 [16], replicated, may hold values from 126976 to 130816, as said below
Outputs:
- query_grads: float32 [4096, 64, 128], P('ctx', 'head')
- key_grads: float32 [4096, 128], P(('ctx', 'head'))
Inputs may be any that keep to these rules, and one draw needn't show every extreme that they name: block_offsets is 126976 plus 256 times a permutation of 0 to 15, so the window covers the last 4096 positions of the context. `index_queries`: every entry is a multiple of 1/8. `index_keys`: every entry is a multiple of 1/8.
All inputs are finite; a program needn't handle non-finite values.
Results may differ from a plain program's by a relative error of at most 0.0029.
Values may be sent and summed in bfloat16 or wider, within the bound.
No kernel may reach another device: no remote copies, remote signals or barrier semaphores. Data moves between devices by JAX's collectives and lax.ppermute only.
A program may use at most 128 MiB of HBM per device.

v0:
```python
import math

import jax
import jax.numpy as jnp
from jax import lax
from jax.sharding import Mesh
from jax.sharding import PartitionSpec as P

CTX = ("ctx_0", "ctx_1", "ctx_2")
HEAD = ("head_0", "head_1")
CTX_HEAD = ("ctx_0", "ctx_1", "ctx_2", "head_0", "head_1")


score_scale = 192.0 ** (-0.5)


def sent_together(arrays, axis, dim, along):
    widths = [a.shape[along] for a in arrays]
    both = jnp.concatenate(arrays, axis=along)
    filled = lax.all_gather(both, axis, axis=dim, tiled=True)
    return tuple(jnp.split(filled, [sum(widths[:k]) for k in range(1, len(widths))], axis=along))


def sent_together_2(arrays, axis, split_dim, concat_dim, along):
    widths = [math.prod(a.shape[along:]) for a in arrays]
    both = jnp.concatenate(
        [a.reshape(*a.shape[:along], w) for a, w in zip(arrays, widths)], axis=along
    )
    filled = lax.all_to_all(both, axis, split_axis=split_dim, concat_axis=concat_dim, tiled=True)
    tiles = jnp.split(filled, [sum(widths[:k]) for k in range(1, len(widths))], axis=along)
    return tuple(
        (b.reshape(*filled.shape[:along], *a.shape[along:]) for a, b in zip(arrays, tiles))
    )


def split_up(array, dim, peers):
    before, after = (array.shape[:dim], array.shape[dim + 1 :])
    return jnp.moveaxis(array.reshape(*before, peers, -1, *after), dim, 0)


def piece_ends(length, count):
    unit = 8 if length >= 8 * count else 1
    return [length // unit * k // count * unit for k in range(1, count)]


def sum_in_order(tiles, axes, sequence):
    shape = [lax.axis_size(a) for a in axes]
    tiles = tiles.reshape(*shape, *tiles.shape[1:])
    tiles = tiles.transpose(*sequence, *range(len(axes), tiles.ndim))
    tiles = tiles.reshape(-1, *tiles.shape[len(axes) :])
    for k in sequence:
        tiles = lax.psum_scatter(tiles, axes[k], scatter_dimension=0, tiled=True)
    return tiles[0]


def sum_all_axes(array, axes, dim):
    tiles = split_up(array, dim, lax.axis_size(axes))
    widest = max(range(1, max(2, tiles.ndim - 1)), key=lambda d: tiles.shape[d])
    count, outs = (len(axes), [])
    for leading, share in enumerate(
        jnp.split(tiles, piece_ends(tiles.shape[widest], count), axis=widest)
    ):
        if share.size:
            sequence = [(leading + k) % count for k in range(count)]
            outs.append(sum_in_order(share, axes, sequence))
    return jnp.concatenate(outs, axis=widest - 1)


def block_width(count):
    width = min(count, 512)
    while count % width:
        width = width - 1
    return width


def table_lookup(block_offsets, index, rows):
    block_ids = lax.iota(jnp.int32, block_offsets.shape[0])
    which = index // rows
    picked = jnp.sum(
        jnp.where(which[:, None] == block_ids[None, :], block_offsets[None, :], 0), axis=1
    )
    return picked + index % rows


def index_scores(queries, weights, keys_all):
    dots = jnp.einsum("rjd,sd->rjs", queries, keys_all, preferred_element_type=jnp.float32)
    partial_logit = jnp.sum(
        jnp.maximum(dots, 0.0) * weights.astype(jnp.float32)[:, :, None], axis=1
    )
    return (dots, partial_logit)


def logit_grads(logit, raw, allowed, lossw):
    target = raw / jnp.sum(raw, axis=1, keepdims=True)
    masked = jnp.where(allowed, logit, jnp.float32(-1e30))
    expo = jnp.where(
        allowed, jnp.exp(masked - jnp.max(masked, axis=1, keepdims=True)), jnp.float32(0.0)
    )
    prob = expo / jnp.sum(expo, axis=1, keepdims=True)
    return lossw[:, None] * (prob - target)


def back_terms(dots, grad, weights, queries, keys_all, iscale):
    coef = jnp.where(
        dots > 0, grad[:, None, :] * weights.astype(jnp.float32)[:, :, None], jnp.float32(0.0)
    ).astype(jnp.bfloat16)
    qgrad = jnp.einsum("rjs,sd->rjd", coef, keys_all, preferred_element_type=jnp.float32) * iscale
    kterm = jnp.einsum("rjs,rjd->sd", coef, queries, preferred_element_type=jnp.float32) * iscale
    return (qgrad, kterm)


def local(
    main_queries,
    latents,
    saved_lse,
    index_queries,
    index_keys,
    head_weights,
    row_weight,
    block_offsets,
):
    rows = main_queries.shape[0]
    local_heads = main_queries.shape[1]
    width_latent = main_queries.shape[2]
    idim = index_keys.shape[1]
    total = rows * block_offsets.shape[0]
    iscale = idim ** (-0.5)
    ctx_index = lax.axis_index(CTX)
    base = ctx_index * rows + lax.iota(jnp.int32, rows)
    q_pos = table_lookup(block_offsets, base, rows)
    flat_queries = main_queries.reshape(rows * local_heads, width_latent)

    def mass_block(lat_block, key_pos):
        scores = jnp.einsum(
            "ql,kl->qk", flat_queries, lat_block, preferred_element_type=jnp.float32
        )
        scores = scores.reshape(rows, local_heads, lat_block.shape[0])
        summed = jnp.sum(jnp.exp(scores * score_scale - saved_lse[:, :, None]), axis=1)
        return jnp.where(key_pos[None, :] <= q_pos[:, None], summed, jnp.float32(0.0))

    masses = jnp.zeros((rows, total), jnp.float32)
    lat_piece, key_piece = sent_together((latents, index_keys), CTX, 0, 1)
    count = lat_piece.shape[0]
    width = block_width(count)

    def one_block(step, masses):
        offset = step * width
        lat_block = lax.dynamic_slice_in_dim(lat_piece, offset, width, 0)
        key_pos = table_lookup(block_offsets, offset + lax.iota(jnp.int32, width), rows)
        part = mass_block(lat_block, key_pos)
        return lax.dynamic_update_slice_in_dim(masses, part, offset, 1)

    masses = lax.fori_loop(0, count // width, one_block, masses)
    k_pos = table_lookup(block_offsets, lax.iota(jnp.int32, total), rows)
    share = rows // lax.axis_size(HEAD)
    head_index = lax.axis_index(HEAD)
    raw = lax.psum_scatter(masses, HEAD, scatter_dimension=0, tiled=True)
    queries, weights = sent_together_2((index_queries, head_weights), HEAD, 0, 1, 2)
    sub_pos = lax.dynamic_slice_in_dim(q_pos, head_index * share, share, 0)
    lossw = lax.dynamic_slice_in_dim(row_weight, head_index * share, share, 0)
    dots, partial_logit = index_scores(queries, weights, key_piece)
    allowed = k_pos[None, :] <= sub_pos[:, None]
    grad = logit_grads(partial_logit * iscale, raw, allowed, lossw)
    row_qgrad, kterm = back_terms(dots, grad, weights, queries, key_piece, iscale)
    query_grads = lax.all_to_all(row_qgrad, HEAD, split_axis=1, concat_axis=0, tiled=True)
    key_grads = sum_all_axes(kterm, CTX_HEAD, 0)
    return (query_grads, key_grads)


def solution(mesh):
    torus = Mesh(
        mesh.devices.reshape(2, 4, 2, 4, 2), ("ctx_0", "ctx_1", "ctx_2", "head_0", "head_1")
    )
    placed = (
        P(CTX, HEAD, None),
        P(CTX, None),
        P(CTX, HEAD),
        P(CTX, HEAD, None),
        P(CTX, None),
        P(CTX, HEAD),
        P(CTX),
        P(),
    )
    return jax.shard_map(
        local,
        mesh=torus,
        in_specs=placed,
        out_specs=(P(CTX, HEAD, None), P(CTX_HEAD, None)),
        check_vma=False,
    )
```

profile of v0, /device:TPU:0, one launch (start us, length us, event | category | flops | bytes accessed | tf_op | source)
XLA Modules:
  0.0 762.6 jit_solution(11143298165912864204)
XLA Ops:
  19.3 35.8 %all-gather.2.cloned.1.call-done = bf16[4096,704]{1,0:T(8,128)(2,1)} async-done(((bf16[256,704]{1,0:T(8,128)(2,1)}), bf16[4096,704]{1,0:T(8,128)(2,1)}) %all-gather.2.cloned.1.call-update) | async-done | bytes 5767184 | tf_op jit(solution)/shard_map/all_gather | solution.py:20
  62.9 191.7 %while.15 = (s32[]{:T(128)}, f32[256,4096]{1,0:T(8,128)}, s32[16]{0:T(128)S(1)}, s32[256]{0:T(256)S(1)}, bf16[4096,576]{1,0:T(8,128)(2,1)}, /*index=5*/bf16[4096...) while((s32[]{:T(128)}, f32[256,4096]{1,0:T(8,128)}, ...), condition=%wide.region_8.9_spmd, body=%wide.region_5.8_spmd.sunk | while | flops 2422380544 | bytes 41055468 | solution.py:153
  62.9 9.4 %multiply_bitcast_fusion.2 = f32[4096,512]{0,1:T(8,128)} fusion(bf16[4096,576]{1,0:T(8,128)(2,1)} %get-tuple-element.301, bf16[4096,576]{1,0:T(8,128)(2,1)} %get-tuple-element.300, s32[]{:T(128)S(6)} %select_n.188), kind=kOutput, calls=%fused_computation.1.clone.1 | convolution fusion | flops 2418016256 | bytes 14286852 | tf_op jit(solution)/shard_map/while/body/eval_jaxpr/ql,kl->qk/dot_general | solution.py:134
  86.9 9.4 %multiply_bitcast_fusion.2 = f32[4096,512]{0,1:T(8,128)} fusion(bf16[4096,576]{1,0:T(8,128)(2,1)} %get-tuple-element.301, bf16[4096,576]{1,0:T(8,128)(2,1)} %get-tuple-element.300, s32[]{:T(128)S(6)} %select_n.188), kind=kOutput, calls=%fused_computation.1.clone.1 | convolution fusion | flops 2418016256 | bytes 14286852 | tf_op jit(solution)/shard_map/while/body/eval_jaxpr/ql,kl->qk/dot_general | solution.py:134
  110.8 9.4 %multiply_bitcast_fusion.2 = f32[4096,512]{0,1:T(8,128)} fusion(bf16[4096,576]{1,0:T(8,128)(2,1)} %get-tuple-element.301, bf16[4096,576]{1,0:T(8,128)(2,1)} %get-tuple-element.300, s32[]{:T(128)S(6)} %select_n.188), kind=kOutput, calls=%fused_computation.1.clone.1 | convolution fusion | flops 2418016256 | bytes 14286852 | tf_op jit(solution)/shard_map/while/body/eval_jaxpr/ql,kl->qk/dot_general | solution.py:134
  134.8 9.4 %multiply_bitcast_fusion.2 = f32[4096,512]{0,1:T(8,128)} fusion(bf16[4096,576]{1,0:T(8,128)(2,1)} %get-tuple-element.301, bf16[4096,576]{1,0:T(8,128)(2,1)} %get-tuple-element.300, s32[]{:T(128)S(6)} %select_n.188), kind=kOutput, calls=%fused_computation.1.clone.1 | convolution fusion | flops 2418016256 | bytes 14286852 | tf_op jit(solution)/shard_map/while/body/eval_jaxpr/ql,kl->qk/dot_general | solution.py:134
  158.8 9.4 %multiply_bitcast_fusion.2 = f32[4096,512]{0,1:T(8,128)} fusion(bf16[4096,576]{1,0:T(8,128)(2,1)} %get-tuple-element.301, bf16[4096,576]{1,0:T(8,128)(2,1)} %get-tuple-element.300, s32[]{:T(128)S(6)} %select_n.188), kind=kOutput, calls=%fused_computation.1.clone.1 | convolution fusion | flops 2418016256 | bytes 14286852 | tf_op jit(solution)/shard_map/while/body/eval_jaxpr/ql,kl->qk/dot_general | solution.py:134
  206.7 9.4 %multiply_bitcast_fusion.2 = f32[4096,512]{0,1:T(8,128)} fusion(bf16[4096,576]{1,0:T(8,128)(2,1)} %get-tuple-element.301, bf16[4096,576]{1,0:T(8,128)(2,1)} %get-tuple-element.300, s32[]{:T(128)S(6)} %select_n.188), kind=kOutput, calls=%fused_computation.1.clone.1 | convolution fusion | flops 2418016256 | bytes 14286852 | tf_op jit(solution)/shard_map/while/body/eval_jaxpr/ql,kl->qk/dot_general | solution.py:134
  230.6 9.4 %multiply_bitcast_fusion.2 = f32[4096,512]{0,1:T(8,128)} fusion(bf16[4096,576]{1,0:T(8,128)(2,1)} %get-tuple-element.301, bf16[4096,576]{1,0:T(8,128)(2,1)} %get-tuple-element.300, s32[]{:T(128)S(6)} %select_n.188), kind=kOutput, calls=%fused_computation.1.clone.1 | convolution fusion | flops 2418016256 | bytes 14286852 | tf_op jit(solution)/shard_map/while/body/eval_jaxpr/ql,kl->qk/dot_general | solution.py:134
  263.3 19.6 %all-to-all-done = bf16[256,8,129]{2,1,0:T(8,128)(2,1)S(1)} async-done(((bf16[256,8,129]{2,1,0:T(8,128)(2,1)}), bf16[256,8,129]{2,1,0:T(8,128)(2,1)S(1)}, u32[]{:S(2)}, u32[]{:S(2)}) %all-to-all-start) | async-done | bytes 528416 | tf_op jit(solution)/shard_map/all_to_all | solution.py:29
  283.4 15.9 %convert_reduce_fusion = (u32[64,4096]{1,0:T(8,128)S(1)}, f32[32,64,4096]{2,1,0:T(8,128)}) fusion(bf16[4096,704]{1,0:T(8,128)(2,1)} %all-gather.2.cloned.1.call-done, bf16[32,64,129]{2,1,0:T(8,128)(2,1)S(1)} %bitcast.66), kind=kOutput, calls=%fused_computation.19 | convolution fusion | flops 2180775936 | bytes 36175872 | tf_op jit(solution)/shard_map/rjd,sd->rjs/dot_general | solution.py:86
  299.3 13.7 %multiply_reduce_fusion = f32[32,4096]{1,0:T(8,128)S(1)} fusion(f32[32,64,4096]{2,1,0:T(8,128)} %get-tuple-element.230, f32[32,64]{1,0:T(8,128)S(1)} %convert_reduce_fusion.1), kind=kLoop, calls=%fused_computation.21 | loop fusion | flops 25034752 | bytes 34086912 | tf_op jit(solution)/shard_map/reduce_sum | solution.py:87
  313.6 36.7 %reduce-scatter.22.cloned.1.call-done = f32[32,4096]{1,0:T(8,128)} async-done(((f32[256,4096]{1,0:T(8,128)}), f32[32,4096]{1,0:T(8,128)}) %reduce-scatter.22.cloned.1.call-update) | async-done | bytes 524304 | tf_op jit(solution)/shard_map/reduce_scatter | solution.py:157
  363.5 18.6 %reduce-scatter.32.cloned.1.call-done = f32[32,6,128]{2,1,0:T(8,128)} async-done(((f32[128,6,128]{2,1,0:T(8,128)}), f32[32,6,128]{2,1,0:T(8,128)}) %reduce-scatter.32.cloned.1.call-update) | async-done | bytes 98320 | tf_op jit(solution)/shard_map/reduce_scatter | solution.py:52
  384.7 20.8 %reduce-scatter.48.cloned.1.call-done = f32[32,6,128]{2,1,0:T(8,128)} async-done(((f32[128,6,128]{2,1,0:T(8,128)}), f32[32,6,128]{2,1,0:T(8,128)}) %reduce-scatter.48.cloned.1.call-update) | async-done | bytes 98320 | tf_op jit(solution)/shard_map/reduce_scatter | solution.py:52
  405.6 19.6 %reduce-scatter.24.cloned.1.call-done = f32[64,6,128]{2,1,0:T(8,128)} async-done(((f32[128,6,128]{2,1,0:T(8,128)}), f32[64,6,128]{2,1,0:T(8,128)}) %reduce-scatter.24.cloned.1.call-update) | async-done | bytes 196624 | tf_op jit(solution)/shard_map/reduce_scatter | solution.py:52
  425.3 13.2 %reduce-scatter.34.cloned.1.call-done = f32[16,6,128]{2,1,0:T(8,128)} async-done(((f32[32,6,128]{2,1,0:T(8,128)}), f32[16,6,128]{2,1,0:T(8,128)}) %reduce-scatter.34.cloned.1.call-update) | async-done | bytes 49168 | tf_op jit(solution)/shard_map/reduce_scatter | solution.py:52
  438.6 14.4 %reduce-scatter.40.cloned.1.call-done = f32[64,7,128]{2,1,0:T(8,128)} async-done(((f32[128,7,128]{2,1,0:T(8,128)}), f32[64,7,128]{2,1,0:T(8,128)}) %reduce-scatter.40.cloned.1.call-update) | async-done | bytes 229392 | tf_op jit(solution)/shard_map/reduce_scatter | solution.py:52
  453.0 18.2 %reduce-scatter.50.cloned.1.call-done = f32[16,6,128]{2,1,0:T(8,128)} async-done(((f32[32,6,128]{2,1,0:T(8,128)}), f32[16,6,128]{2,1,0:T(8,128)}) %reduce-scatter.50.cloned.1.call-update) | async-done | bytes 49168 | tf_op jit(solution)/shard_map/reduce_scatter | solution.py:52
  493.6 22.2 %reduce-scatter.36.cloned.1.call-done = f32[4,6,128]{2,1,0:T(8,128)} async-done(((f32[16,6,128]{2,1,0:T(8,128)}), f32[4,6,128]{2,1,0:T(8,128)}) %reduce-scatter.36.cloned.1.call-update) | async-done | bytes 12304 | tf_op jit(solution)/shard_map/reduce_scatter | solution.py:52
  515.8 22.7 %reduce-scatter.42.cloned.1.call-done = f32[16,7,128]{2,1,0:T(8,128)} async-done(((f32[64,7,128]{2,1,0:T(8,128)}), f32[16,7,128]{2,1,0:T(8,128)}) %reduce-scatter.42.cloned.1.call-update) | async-done | bytes 57360 | tf_op jit(solution)/shard_map/reduce_scatter | solution.py:52
  538.6 14.4 %reduce-scatter.52.cloned.1.call-done = f32[8,6,128]{2,1,0:T(8,128)} async-done(((f32[16,6,128]{2,1,0:T(8,128)}), f32[8,6,128]{2,1,0:T(8,128)}) %reduce-scatter.52.cloned.1.call-update) | async-done | bytes 24592 | tf_op jit(solution)/shard_map/reduce_scatter | solution.py:52
  553.1 22.2 %reduce-scatter.56.cloned.1.call-done = f32[64,7,128]{2,1,0:T(8,128)} async-done(((f32[128,7,128]{2,1,0:T(8,128)}), f32[64,7,128]{2,1,0:T(8,128)}) %reduce-scatter.56.cloned.1.call-update) | async-done | bytes 229392 | tf_op jit(solution)/shard_map/reduce_scatter | solution.py:52
  575.3 11.3 %reduce-scatter.28.cloned.1.call-done = f32[8,6,128]{2,1,0:T(8,128)} async-done(((f32[16,6,128]{2,1,0:T(8,128)}), f32[8,6,128]{2,1,0:T(8,128)}) %reduce-scatter.28.cloned.1.call-update) | async-done | bytes 24592 | tf_op jit(solution)/shard_map/reduce_scatter | solution.py:52
  591.2 13.0 %reduce-scatter.38.cloned.1.call-done = f32[2,6,128]{2,1,0:T(8,128)} async-done(((f32[4,6,128]{2,1,0:T(8,128)}), f32[2,6,128]{2,1,0:T(8,128)}) %reduce-scatter.38.cloned.1.call-update) | async-done | bytes 6160 | tf_op jit(solution)/shard_map/reduce_scatter | solution.py:52
  609.3 10.3 %reduce-scatter.44.cloned.1.call-done = f32[8,7,128]{2,1,0:T(8,128)} async-done(((f32[16,7,128]{2,1,0:T(8,128)}), f32[8,7,128]{2,1,0:T(8,128)}) %reduce-scatter.44.cloned.1.call-update) | async-done | bytes 28688 | tf_op jit(solution)/shard_map/reduce_scatter | solution.py:52
  620.3 21.0 %reduce-scatter.54.cloned.1.call-done = f32[2,6,128]{2,1,0:T(8,128)} async-done(((f32[8,6,128]{2,1,0:T(8,128)}), f32[2,6,128]{2,1,0:T(8,128)}) %reduce-scatter.54.cloned.1.call-update) | async-done | bytes 6160 | tf_op jit(solution)/shard_map/reduce_scatter | solution.py:52
  643.9 13.7 %reduce-scatter.58.cloned.1.call-done = f32[32,7,128]{2,1,0:T(8,128)} async-done(((f32[64,7,128]{2,1,0:T(8,128)}), f32[32,7,128]{2,1,0:T(8,128)}) %reduce-scatter.58.cloned.1.call-update) | async-done | bytes 114704 | tf_op jit(solution)/shard_map/reduce_scatter | solution.py:52
  658.3 22.8 %reduce-scatter.30.cloned.1.call-done = f32[2,6,128]{2,1,0:T(8,128)} async-done(((f32[8,6,128]{2,1,0:T(8,128)}), f32[2,6,128]{2,1,0:T(8,128)}) %reduce-scatter.30.cloned.1.call-update) | async-done | bytes 6160 | tf_op jit(solution)/shard_map/reduce_scatter | solution.py:52
  695.6 17.5 %all-reduce.2 = f32[4,7,128]{2,1,0:T(8,128)S(1)} all-reduce(f32[4,7,128]{2,1,0:T(8,128)} %reduce-scatter.46.cloned.1.call-done), channel_id=17, replica_groups=mesh['ctx_0'=2,'ctx_1'=4,'ctx_2'=2,'head_0'=4,'head_1'=2] {'ctx_1'}, use_global_device_ids=true, to_apply=%region_25.26.clone | all-reduce | flops 3584 | bytes 28672
  720.1 11.4 %reduce-scatter.62.cloned.1.call-done = f32[4,7,128]{2,1,0:T(8,128)} async-done(((f32[8,7,128]{2,1,0:T(8,128)}), f32[4,7,128]{2,1,0:T(8,128)}) %reduce-scatter.62.cloned.1.call-update) | async-done | bytes 14352 | tf_op jit(solution)/shard_map/reduce_scatter | solution.py:52
  731.5 17.7 %all-reduce.4 = f32[4,7,128]{2,1,0:T(8,128)S(1)} all-reduce(f32[4,7,128]{2,1,0:T(8,128)} %reduce-scatter.62.cloned.1.call-done), channel_id=27, replica_groups=mesh['ctx_0'=2,'ctx_1'=4,'ctx_2'=2,'head_0'=4,'head_1'=2] {'head_0'}, use_global_device_ids=true, to_apply=%region_35.36.clone | all-reduce | flops 3584 | bytes 28672
  (167 shorter events, 235.2 us)
Async XLA Ops:
  7.2 12.1 %copy-start.2 = (s32[16]{0:T(128)S(1)}, s32[16]{0:T(128)}, u32[]{:S(2)}) copy-start(s32[16]{0:T(128)} %param.17) | copy-start | bytes 196
  7.2 48.0 %all-gather.2.cloned.1.call-start = ((), (), s32[]{:S(2)}) async-start(), calls=%async_computation.23 | async-start | bytes 6684672 | tf_op jit(solution)/shard_map/all_gather | solution.py:20
  10.1 340.2 %reduce-scatter.22.cloned.1.call-start = ((), (), s32[]{:S(2)}) async-start(), calls=%async_computation.24 | async-start | bytes 4718592 | tf_op jit(solution)/shard_map/reduce_scatter | solution.py:157
  62.9 191.7 %copy-start.4 = (bf16[256,8]{0,1:T(8,128)(2,1)S(1)}, bf16[256,8]{0,1:T(8,128)(2,1)}, u32[]{:S(2)}) copy-start(bf16[256,8]{0,1:T(8,128)(2,1)} %param.15) | copy-start | bytes 12292
  62.9 192.1 %copy-start.1 = (bf16[256,8,128]{2,1,0:T(8,128)(2,1)S(1)}, bf16[256,8,128]{2,1,0:T(8,128)(2,1)}, u32[]{:S(2)}) copy-start(bf16[256,8,128]{2,1,0:T(8,128)(2,1)} %param.13) | copy-start | bytes 1572868
  256.2 26.8 %all-to-all-start = ((bf16[256,8,129]{2,1,0:T(8,128)(2,1)}), bf16[256,8,129]{2,1,0:T(8,128)(2,1)S(1)}, u32[]{:S(2)}, u32[]{:S(2)}) async-start(bf16[256,8,129]{2,1,0:T(8,128)(2,1)} %pad_maximum_fusion), calls=%async_computation | async-start | bytes 2097152 | tf_op jit(solution)/shard_map/all_to_all | solution.py:29
  262.8 119.4 %reduce-scatter.32.cloned.1.call-start = ((), (), s32[]{:S(2)}) async-start(), calls=%async_computation.29 | async-start | bytes 655360 | tf_op jit(solution)/shard_map/reduce_scatter | solution.py:52
  362.0 43.5 %reduce-scatter.48.cloned.1.call-start = ((), (), s32[]{:S(2)}) async-start(), calls=%async_computation.37 | async-start | bytes 655360 | tf_op jit(solution)/shard_map/reduce_scatter | solution.py:52
  362.9 62.3 %reduce-scatter.24.cloned.1.call-start = ((), (), s32[]{:S(2)}) async-start(), calls=%async_computation.25 | async-start | bytes 786432 | tf_op jit(solution)/shard_map/reduce_scatter | solution.py:52
  363.5 75.0 %reduce-scatter.34.cloned.1.call-start = ((), (), s32[]{:S(2)}) async-start(), calls=%async_computation.30 | async-start | bytes 196608 | tf_op jit(solution)/shard_map/reduce_scatter | solution.py:52
  382.2 70.8 %reduce-scatter.40.cloned.1.call-start = ((), (), s32[]{:S(2)}) async-start(), calls=%async_computation.33 | async-start | bytes 786432 | tf_op jit(solution)/shard_map/reduce_scatter | solution.py:52
  384.6 86.6 %reduce-scatter.50.cloned.1.call-start = ((), (), s32[]{:S(2)}) async-start(), calls=%async_computation.38 | async-start | bytes 196608 | tf_op jit(solution)/shard_map/reduce_scatter | solution.py:52
  405.5 87.9 %reduce-scatter.26.cloned.1.call-start = ((), (), s32[]{:S(2)}) async-start(), calls=%async_computation.26 | async-start | bytes 327680 | tf_op jit(solution)/shard_map/reduce_scatter | solution.py:52
  425.2 90.5 %reduce-scatter.36.cloned.1.call-start = ((), (), s32[]{:S(2)}) async-start(), calls=%async_computation.31 | async-start | bytes 81920 | tf_op jit(solution)/shard_map/reduce_scatter | solution.py:52
  438.5 100.0 %reduce-scatter.42.cloned.1.call-start = ((), (), s32[]{:S(2)}) async-start(), calls=%async_computation.34 | async-start | bytes 327680 | tf_op jit(solution)/shard_map/reduce_scatter | solution.py:52
  453.0 100.0 %reduce-scatter.52.cloned.1.call-start = ((), (), s32[]{:S(2)}) async-start(), calls=%async_computation.39 | async-start | bytes 98304 | tf_op jit(solution)/shard_map/reduce_scatter | solution.py:52
  471.3 103.9 %reduce-scatter.56.cloned.1.call-start = ((), (), s32[]{:S(2)}) async-start(), calls=%async_computation.41 | async-start | bytes 786432 | tf_op jit(solution)/shard_map/reduce_scatter | solution.py:52
  472.4 114.2 %copy-start.10 = (u32[128]{0:T(128)S(1)}, u32[128]{0:T(128)}, u32[]{:S(2)}) copy-start(u32[128]{0:T(128)} %constant.208) | copy-start | bytes 1540
  472.4 114.8 %copy-start.9 = (u32[128]{0:T(128)S(1)}, u32[128]{0:T(128)}, u32[]{:S(2)}) copy-start(u32[128]{0:T(128)} %constant.200) | copy-start | bytes 1540
  472.5 115.4 %copy-start.8 = (u32[128]{0:T(128)S(1)}, u32[128]{0:T(128)}, u32[]{:S(2)}) copy-start(u32[128]{0:T(128)} %constant.212) | copy-start | bytes 1540
  472.5 116.0 %copy-start.7 = (u32[128]{0:T(128)S(1)}, u32[128]{0:T(128)}, u32[]{:S(2)}) copy-start(u32[128]{0:T(128)} %constant.204) | copy-start | bytes 1540
  472.5 116.5 %copy-start.6 = (u32[128]{0:T(128)S(1)}, u32[128]{0:T(128)}, u32[]{:S(2)}) copy-start(u32[128]{0:T(128)} %constant.196) | copy-start | bytes 1540
  480.9 108.7 %all-to-all-start.1 = ((f32[32,64,128]{2,0,1:T(8,128)}), f32[32,64,128]{2,0,1:T(8,128)S(1)}, u32[]{:S(2)}, u32[]{:S(2)}) async-start(f32[32,64,128]{2,0,1:T(8,128)} %copy.49), calls=%async_computation.2 | async-start | bytes 2097152 | tf_op jit(solution)/shard_map/all_to_all | solution.py:165
  485.1 101.5 %reduce-scatter.28.cloned.1.call-start = ((), (), s32[]{:S(2)}) async-start(), calls=%async_computation.27 | async-start | bytes 98304 | tf_op jit(solution)/shard_map/reduce_scatter | solution.py:52
  493.5 110.7 %reduce-scatter.38.cloned.1.call-start = ((), (), s32[]{:S(2)}) async-start(), calls=%async_computation.32 | async-start | bytes 24576 | tf_op jit(solution)/shard_map/reduce_scatter | solution.py:52
  515.8 103.8 %reduce-scatter.44.cloned.1.call-start = ((), (), s32[]{:S(2)}) async-start(), calls=%async_computation.35 | async-start | bytes 98304 | tf_op jit(solution)/shard_map/reduce_scatter | solution.py:52
  538.5 102.8 %reduce-scatter.54.cloned.1.call-start = ((), (), s32[]{:S(2)}) async-start(), calls=%async_computation.40 | async-start | bytes 40960 | tf_op jit(solution)/shard_map/reduce_scatter | solution.py:52
  553.0 104.6 %reduce-scatter.58.cloned.1.call-start = ((), (), s32[]{:S(2)}) async-start(), calls=%async_computation.42 | async-start | bytes 393216 | tf_op jit(solution)/shard_map/reduce_scatter | solution.py:52
  575.2 105.9 %reduce-scatter.30.cloned.1.call-start = ((), (), s32[]{:S(2)}) async-start(), calls=%async_computation.28 | async-start | bytes 40960 | tf_op jit(solution)/shard_map/reduce_scatter | solution.py:52
  586.6 109.0 %reduce-scatter.46.cloned.1.call-start = ((), (), s32[]{:S(2)}) async-start(), calls=%async_computation.36 | async-start | bytes 49152 | tf_op jit(solution)/shard_map/reduce_scatter | solution.py:52
  619.7 99.8 %reduce-scatter.60.cloned.1.call-start = ((), (), s32[]{:S(2)}) async-start(), calls=%async_computation.43 | async-start | bytes 163840 | tf_op jit(solution)/shard_map/reduce_scatter | solution.py:52
  657.6 73.8 %reduce-scatter.62.cloned.1.call-start = ((), (), s32[]{:S(2)}) async-start(), calls=%async_computation.44 | async-start | bytes 49152 | tf_op jit(solution)/shard_map/reduce_scatter | solution.py:52
  (3 other events, 21.8 us)
Sparse Core Ops, SparseCore 0:
  10.3 44.8 all-gather.1
  254.7 95.5 reduce-scatter.21
  362.1 20.0 reduce-scatter.31
  384.4 21.0 reduce-scatter.47
  408.3 16.8 reduce-scatter.23
  427.5 10.9 reduce-scatter.33
  441.0 11.9 reduce-scatter.39
  455.3 15.9 reduce-scatter.49
  473.6 19.7 reduce-scatter.25
  495.8 19.9 reduce-scatter.35
  518.2 20.3 reduce-scatter.41
  540.8 12.1 reduce-scatter.51
  555.5 19.7 reduce-scatter.55
  577.4 9.1 reduce-scatter.27
  588.7 15.4 reduce-scatter.37
  606.4 13.2 reduce-scatter.43
  621.8 19.4 reduce-scatter.53
  643.6 13.9 reduce-scatter.57
  659.9 21.1 reduce-scatter.29
  683.4 12.1 reduce-scatter.45
  698.1 21.3 reduce-scatter.59
  721.8 9.6 reduce-scatter.61
where the time goes:
time: 765 us; the launch traced here: 763 us
  waiting for transfers between devices  405 us (53%)
  local copies, waits for them, and re-layouts  113 us (15%)
  matrix products  104 us (14%)
  other arithmetic  64.9 us (8%)
  blocking collectives  49.5 us (6%)
  between operations  14.6 us (2%)
  starting transfers between devices  12.1 us (2%)
    reduce_scatter x20, waiting for transfers between devices, sum_in_order(): tiles = lax.psum_scatter(tiles, axes[k], scatter_dimension=0, tiled=True)  312 us
    dot_general x8, matrix products, mass_block(): jnp.einsum('ql,kl->qk', flat_queries, lat_block, preferred_element_type=j...  75 us
    mul x8, local copies, waits for them, and re-layouts, mass_block(): scores * score_scale - saved_lse[:, :, None]  71.9 us
    unnamed x5, blocking collectives  49.5 us
    reduce_scatter x1, waiting for transfers between devices, local(): raw = lax.psum_scatter(masses, HEAD, scatter_dimension=0, tiled=True)  36.7 us
    reduce_sum x8, other arithmetic, mass_block(): jnp.sum(jnp.exp(scores * score_scale - saved_lse[:, :, None]), axis=1)  36.3 us
    all_gather x1, waiting for transfers between devices, sent_together(): filled = lax.all_gather(both, axis, axis=dim, tiled=True)  35.8 us
    all_to_all x1, waiting for transfers between devices, sent_together_2(): lax.all_to_all(both, axis, split_axis=split_dim, concat_axis=concat_dim,...  19.6 us
  transfers between devices with their start and end apart: 24, of which 23 were waited for; matrix products, arithmetic and copies ran while one was open for 8% of the time, Pallas kernels for 0%

commit v1 on v0

v1 whole, which is shorter than its diff:
```python
import functools

import jax
import jax.numpy as jnp
from jax import lax
from jax.experimental import pallas as pl
from jax.experimental.pallas import tpu as pltpu
from jax.sharding import Mesh
from jax.sharding import PartitionSpec as P

CTX = ("ctx_0", "ctx_1", "ctx_2")
HEAD = ("head_0", "head_1")
ALL = CTX + HEAD

ROWS = 256
LATENT = 576
IDIM = 128
HEADS_DEV = 16
PEERS = 8
SHARE = ROWS // PEERS
BLOCKS = 16
TOTAL = BLOCKS * ROWS
PAD = 16
LOG2E = 1.4426950408889634
SCORE = 192.0 ** -0.5
ISCALE = IDIM ** -0.5
VMEM = 48 * 2**20

ORDER = (
    (0, 0, 0), (0, 0, 1),
    (1, 0, 0), (0, 3, 0), (0, 1, 0), (1, 0, 1), (0, 3, 1), (0, 1, 1),
    (1, 3, 0), (1, 1, 0), (0, 2, 0), (1, 3, 1), (1, 1, 1), (0, 2, 1),
    (1, 2, 0), (1, 2, 1),
)


def mass_kernel(first, count, hstep, ids, table, q_ref, lse_ref, *refs):
    blocks, out_ref, acc = refs[:count], refs[count], refs[count + 1]
    step = pl.program_id(0)

    @pl.when(step == 0)
    def _():
        acc[...] = jnp.zeros_like(acc)

    for b in range(count):
        lat = blocks[b][:, IDIM : IDIM + LATENT]
        rows = slice(b * ROWS, (b + 1) * ROWS)
        part = None
        for i in range(hstep):
            s = jnp.dot(lat, q_ref[i], preferred_element_type=jnp.float32)
            lse = lse_ref[pl.ds(step * hstep + i, 1), :] * jnp.float32(LOG2E)
            e = jnp.exp2(s * jnp.float32(SCORE * LOG2E) - lse)
            part = e if part is None else part + e
        acc[rows, :] += part

    @pl.when(step == pl.num_programs(0) - 1)
    def _():
        q_pos = table[ids[0]] + lax.broadcasted_iota(jnp.int32, (ROWS, ROWS), 0)
        for b in range(count):
            k_pos = table[ids[first + b]] + lax.broadcasted_iota(jnp.int32, (ROWS, ROWS), 1)
            rows = slice(b * ROWS, (b + 1) * ROWS)
            mass = jnp.where(k_pos <= q_pos, acc[rows, :].T, jnp.float32(0.0))
            out_ref[:, rows] = mass.astype(jnp.bfloat16)


def mass_call(ids, table, q_t, lse_t, blocks, first, hstep=4):
    count = len(blocks)
    width = blocks[0].shape[1]
    return pl.pallas_call(
        functools.partial(mass_kernel, first, count, hstep),
        out_shape=jax.ShapeDtypeStruct((ROWS, count * ROWS), jnp.bfloat16),
        grid_spec=pltpu.PrefetchScalarGridSpec(
            num_scalar_prefetch=2,
            grid=(HEADS_DEV // hstep,),
            in_specs=[
                pl.BlockSpec((hstep, LATENT, ROWS), lambda h, *_: (h, 0, 0)),
                pl.BlockSpec((HEADS_DEV, ROWS), lambda h, *_: (0, 0)),
            ]
            + [pl.BlockSpec((ROWS, width), lambda h, *_: (0, 0))] * count,
            out_specs=pl.BlockSpec((ROWS, count * ROWS), lambda h, *_: (0, 0)),
            scratch_shapes=[pltpu.VMEM((count * ROWS, ROWS), jnp.float32)],
        ),
        compiler_params=pltpu.CompilerParams(vmem_limit_bytes=VMEM),
        cost_estimate=pl.CostEstimate(
            flops=2 * HEADS_DEV * ROWS * ROWS * count * LATENT * 4 // 3,
            bytes_accessed=HEADS_DEV * ROWS * LATENT * 2 + count * ROWS * (width + ROWS) * 2,
            transcendentals=HEADS_DEV * ROWS * ROWS * count,
        ),
        name="mass_%d" % first,
    )(ids, table, q_t, lse_t, *blocks)


def logit_kernel(qw_ref, *refs):
    blocks = refs[:BLOCKS]
    logit_ref, keys_ref, wide_ref = refs[BLOCKS:]
    for b in range(BLOCKS):
        keys_ref[b * ROWS : (b + 1) * ROWS, :] = blocks[b][...]
    for h in range(PEERS):
        w = qw_ref[h, ROWS : ROWS + PAD, :].astype(jnp.float32)
        for i in range(2):
            wide_ref[h, i * IDIM : (i + 1) * IDIM, :] = jnp.broadcast_to(
                w[i : i + 1, :], (IDIM, IDIM)
            ).T

    @pl.loop(0, BLOCKS)
    def _(b):
        keys = keys_ref[pl.ds(pl.multiple_of(b * ROWS, ROWS), ROWS), :]
        acc = [None, None]
        for h in range(PEERS):
            dots = lax.dot_general(
                qw_ref[h, :ROWS, :], keys, (((1,), (1,)), ((), ())),
                preferred_element_type=jnp.float32,
            )
            w = wide_ref[h]
            for i in range(2):
                y = jnp.maximum(dots[:, i * IDIM : (i + 1) * IDIM], 0.0) * w
                acc[i] = y if acc[i] is None else acc[i] + y
        for i in range(2):
            logit_ref[:, pl.ds(pl.multiple_of(b * ROWS + i * IDIM, IDIM), IDIM)] = jnp.sum(
                acc[i].reshape(SHARE, PEERS, IDIM), axis=1
            )


def logit_call(qw, blocks):
    return pl.pallas_call(
        logit_kernel,
        out_shape=(
            jax.ShapeDtypeStruct((SHARE, TOTAL), jnp.float32),
            jax.ShapeDtypeStruct((TOTAL, IDIM), jnp.bfloat16),
            jax.ShapeDtypeStruct((PEERS, ROWS, IDIM), jnp.float32),
        ),
        grid=(1,),
        in_specs=[pl.BlockSpec(qw.shape, lambda i: (0, 0, 0))]
        + [pl.BlockSpec((ROWS, IDIM), lambda i: (0, 0))] * BLOCKS,
        out_specs=(
            pl.BlockSpec((SHARE, TOTAL), lambda i: (0, 0)),
            pl.BlockSpec((TOTAL, IDIM), lambda i: (0, 0)),
            pl.BlockSpec((PEERS, ROWS, IDIM), lambda i: (0, 0, 0)),
        ),
        compiler_params=pltpu.CompilerParams(vmem_limit_bytes=VMEM),
        cost_estimate=pl.CostEstimate(
            flops=4 * PEERS * ROWS * TOTAL * IDIM, bytes_accessed=4 * 2**20, transcendentals=0
        ),
        name="logit",
    )(qw, *blocks)


def grad_kernel(chunks, ids, table, qw_ref, logit_ref, keys_ref, wide_ref, loss_ref, *refs):
    raws = refs[: len(chunks)]
    qgrad_ref, kterm_ref, grad, raw, q_t, acc = refs[len(chunks) :]
    sub = ids[BLOCKS] * SHARE
    q_pos = table[ids[0]] + sub + lax.broadcasted_iota(jnp.int32, (SHARE, ROWS), 0)
    peak = None
    mass = None
    start = 0
    for ref, count in zip(raws, chunks):
        for b in range(count):
            cols = slice((start + b) * ROWS, (start + b + 1) * ROWS)
            here = slice(b * ROWS, (b + 1) * ROWS)
            part = ref[0, :, here].astype(jnp.float32)
            for p in range(1, PEERS):
                part = part + ref[p, :, here].astype(jnp.float32)
            raw[:, cols] = part
            mass = part if mass is None else mass + part
            k_pos = table[ids[start + b]] + lax.broadcasted_iota(jnp.int32, (SHARE, ROWS), 1)
            masked = jnp.where(
                k_pos <= q_pos, logit_ref[:, cols] * jnp.float32(ISCALE), jnp.float32(-1e30)
            )
            grad[:, cols] = masked
            peak = masked if peak is None else jnp.maximum(peak, masked)
        start += count
    peak = jnp.max(peak, axis=1, keepdims=True)
    loss = loss_ref[:, :1]
    mass = loss / jnp.sum(mass, axis=1, keepdims=True)
    total = None
    for b in range(BLOCKS):
        cols = slice(b * ROWS, (b + 1) * ROWS)
        e = jnp.exp(grad[:, cols] - peak)
        grad[:, cols] = e
        total = e if total is None else total + e
    total = loss / jnp.sum(total, axis=1, keepdims=True)
    for b in range(BLOCKS):
        cols = slice(b * ROWS, (b + 1) * ROWS)
        grad[:, cols] = grad[:, cols] * total - raw[:, cols] * mass
    for h in range(PEERS):
        q_t[h] = qw_ref[h, :ROWS, :].T
    acc[...] = jnp.zeros_like(acc)

    @pl.loop(0, BLOCKS)
    def _(b):
        rows = pl.ds(pl.multiple_of(b * ROWS, ROWS), ROWS)
        keys = keys_ref[rows, :]
        g = grad[:, rows]
        g = jnp.broadcast_to(g[:, None, :], (SHARE, PEERS, ROWS)).reshape(ROWS, ROWS)
        kterm = None
        for h in range(PEERS):
            dots = lax.dot_general(
                qw_ref[h, :ROWS, :], keys, (((1,), (1,)), ((), ())),
                preferred_element_type=jnp.float32,
            )
            w = wide_ref[h]
            w = jnp.concatenate([w, w], axis=1)
            coef = jnp.where(dots > 0, g * w, jnp.float32(0.0)).astype(jnp.bfloat16)
            acc[h] += jnp.dot(coef, keys, preferred_element_type=jnp.float32)
            part = jnp.dot(q_t[h], coef, preferred_element_type=jnp.float32)
            kterm = part if kterm is None else kterm + part
        kterm = (kterm * jnp.float32(ISCALE)).T
        place = pl.ds(pl.multiple_of(ids[b] * ROWS, ROWS), ROWS)
        kterm_ref[place, :] = kterm.astype(kterm_ref.dtype)

    qgrad_ref[...] = (acc[...] * jnp.float32(ISCALE)).astype(qgrad_ref.dtype)


def grad_call(ids, table, qw, logit, keys, wide, loss, raws):
    chunks = tuple(r.shape[2] // ROWS for r in raws)
    whole = lambda a: pl.BlockSpec(a.shape, lambda i, *_, n=a.ndim: (0,) * n)
    operands = (qw, logit, keys, wide, loss) + tuple(raws)
    return pl.pallas_call(
        functools.partial(grad_kernel, chunks),
        out_shape=(
            jax.ShapeDtypeStruct((PEERS, ROWS, IDIM), jnp.bfloat16),
            jax.ShapeDtypeStruct((TOTAL, IDIM), jnp.bfloat16),
        ),
        grid_spec=pltpu.PrefetchScalarGridSpec(
            num_scalar_prefetch=2,
            grid=(1,),
            in_specs=[whole(a) for a in operands],
            out_specs=(
                pl.BlockSpec((PEERS, ROWS, IDIM), lambda i, *_: (0, 0, 0)),
                pl.BlockSpec((TOTAL, IDIM), lambda i, *_: (0, 0)),
            ),
            scratch_shapes=[
                pltpu.VMEM((SHARE, TOTAL), jnp.float32),
                pltpu.VMEM((SHARE, TOTAL), jnp.float32),
                pltpu.VMEM((PEERS, IDIM, ROWS), jnp.bfloat16),
                pltpu.VMEM((PEERS, ROWS, IDIM), jnp.float32),
            ],
        ),
        compiler_params=pltpu.CompilerParams(vmem_limit_bytes=VMEM),
        cost_estimate=pl.CostEstimate(
            flops=12 * PEERS * ROWS * TOTAL * IDIM, bytes_accessed=8 * 2**20, transcendentals=0
        ),
        name="grads",
    )(ids, table, *operands)


def shift(array, axis, size, by):
    return lax.ppermute(array, axis, [(i, (i + by) % size) for i in range(size)])


def local(
    main_queries, latents, saved_lse, index_queries, index_keys, head_weights, row_weight,
    block_offsets,
):
    c0, c1, c2 = (lax.axis_index(a) for a in CTX)
    head = lax.axis_index(HEAD)
    ids = [(c0 ^ a) * 8 + ((c1 + b) & 3) * 2 + (c2 ^ c) for a, b, c in ORDER]
    ids = jnp.stack([i.astype(jnp.int32) for i in ids + [head]])

    own = jnp.concatenate([index_keys, latents], axis=1)
    core = functools.partial(shift, axis="ctx_2", size=2, by=1)
    up = functools.partial(shift, axis="ctx_1", size=4, by=1)
    down = functools.partial(shift, axis="ctx_1", size=4, by=-1)
    side = functools.partial(shift, axis="ctx_0", size=2, by=1)

    weights = head_weights.reshape(PEERS, 2, IDIM)
    weights = jnp.pad(weights, ((0, 0), (0, PAD - 2), (0, 0)))
    qw = jnp.concatenate([index_queries.reshape(PEERS, ROWS, IDIM), weights], axis=1)

    pair = core(own)
    z, yp, ym = side(own), up(own), down(own)
    pz, pyp, pym = core(z), core(yp), core(ym)
    zyp, zym, y2 = up(z), down(z), up(yp)
    pzyp, pzym, py2 = core(zyp), core(zym), core(y2)
    zy2 = down(zym)
    pzy2 = core(zy2)
    qw = lax.all_to_all(qw, HEAD, 0, 0, tiled=True)

    q_t = jnp.transpose(main_queries, (1, 2, 0))
    lse_t = saved_lse.T
    mass = functools.partial(mass_call, ids, block_offsets, q_t, lse_t)

    def exchange(parts):
        m = jnp.concatenate(parts, axis=1).reshape(PEERS, SHARE, -1)
        return lax.all_to_all(m, HEAD, 0, 0, tiled=True)

    raw_0 = exchange([mass([own, pair], 0), mass([z, yp, ym, pz, pyp, pym], 2)])
    raw_1 = exchange([mass([zyp, zym, y2, pzyp, pzym, py2], 8), mass([zy2, pzy2], 14)])

    blocks = [own, pair, z, yp, ym, pz, pyp, pym, zyp, zym, y2, pzyp, pzym, py2, zy2, pzy2]
    logit, keys, wide = logit_call(qw, blocks)
    loss = lax.dynamic_slice_in_dim(row_weight, head * SHARE, SHARE, 0)
    loss = jnp.broadcast_to(loss[:, None], (SHARE, IDIM))
    qgrad, kterm = grad_call(ids, block_offsets, qw, logit, keys, wide, loss, (raw_0, raw_1))

    qgrad = lax.all_to_all(qgrad, HEAD, 0, 0, tiled=True)
    query_grads = qgrad.reshape(ROWS, PEERS, IDIM).astype(jnp.float32)
    kterm = lax.all_to_all(kterm.reshape(BLOCKS * PEERS, SHARE, IDIM), ALL, 0, 0, tiled=True)
    key_grads = jnp.sum(kterm.astype(jnp.float32), axis=0)
    return query_grads, key_grads


def solution(mesh):
    torus = Mesh(mesh.devices.reshape(2, 4, 2, 4, 2), ALL)
    placed = (
        P(CTX, HEAD, None), P(CTX, None), P(CTX, HEAD), P(CTX, HEAD, None), P(CTX, None),
        P(CTX, HEAD), P(CTX), P(),
    )
    return jax.shard_map(
        local,
        mesh=torus,
        in_specs=placed,
        out_specs=(P(CTX, HEAD, None), P(ALL, None)),
        check_vma=False,
    )
```

time: 765 us -> 176 us (0.23)
  waiting for transfers between devices: 405 us -> 26.4 us
  matrix products: 104 us -> 0 us
  local copies, waits for them, and re-layouts: 113 us -> 12.5 us
  Pallas kernels: 0 us -> 74.5 us
  other arithmetic: 64.9 us -> 6.96 us
  blocking collectives: 49.5 us -> 14.7 us
  starting transfers between devices: 12.1 us -> 39.3 us
  between operations: 14.6 us -> 0.82 us
    reduce_scatter x21 -> x0, waiting for transfers between devices: 349 us -> none  [the longest x20 312 us: sum_in_order(): tiles = lax.psum_scatter(tiles, axes[k], scatter_dimension=0, tiled=True)]
    dot_general x11 -> x0, matrix products: 104 us -> none  [the longest x8 75 us: mass_block(): jnp.einsum('ql,kl->qk', flat_queries, lat_block, preferred_element_type=j...]
    pallas_call x0 -> x6, Pallas kernels: none -> 74.5 us  [the longest x4 37.3 us: mass_call(): pl.pallas_call(functools.partial(mass_kernel, first, count, hstep), out_s...]
    mul x9 -> x0, local copies, waits for them, and re-layouts: 73.5 us -> none  [the longest x8 71.9 us: mass_block(): scores * score_scale - saved_lse[:, :, None]]
    reduce_sum x21 -> x1, other arithmetic: 52.4 us -> 0.8 us  [local(): key_grads = jnp.sum(kterm.astype(jnp.float32), axis=0)]
    unnamed x5 -> x0, blocking collectives: 49.5 us -> none
    all_gather x1 -> x0, waiting for transfers between devices: 35.8 us -> none  [sent_together(): filled = lax.all_gather(both, axis, axis=dim, tiled=True)]
    all_to_all x2 -> x4, starting transfers between devices: 10.9 us -> 26.4 us  [the longest x2 14.4 us: exchange(): return lax.all_to_all(m, HEAD, 0, 0, tiled=True)]
  transfers between devices with their start and end apart: 24 -> 19, of which waited for: 23 -> 3; matrix products, arithmetic and copies ran while one was open for 8% -> 4% of each run, Pallas kernels for 0% -> 27%
where the time goes in v1:
time: 176 us; the launch traced here: 175 us
  Pallas kernels  74.5 us (42%)
  starting transfers between devices  39.3 us (22%)
  waiting for transfers between devices  26.4 us (15%)
  blocking collectives  14.7 us (8%)
  local copies, waits for them, and re-layouts  12.5 us (7%)
  other arithmetic  6.96 us (4%)
    pallas_call x4, Pallas kernels, mass_call(): pl.pallas_call(functools.partial(mass_kernel, first, count, hstep), out_s...  37.3 us
    pallas_call x1, Pallas kernels, grad_call(): pl.pallas_call(functools.partial(grad_kernel, chunks), out_shape=(jax.Sha...  26.7 us
    all_to_all x1, waiting for transfers between devices, local(): lax.all_to_all(kterm.reshape(BLOCKS * PEERS, SHARE, IDIM), ALL, 0, 0, til...  17.3 us
    all_to_all x1, blocking collectives, local(): qgrad = lax.all_to_all(qgrad, HEAD, 0, 0, tiled=True)  14.7 us
    all_to_all x2, starting transfers between devices, exchange(): return lax.all_to_all(m, HEAD, 0, 0, tiled=True)  14.4 us
    ppermute x15, starting transfers between devices, shift(): lax.ppermute(array, axis, [(i, (i + by) % size) for i in range(size)])  12.9 us
    unnamed x30, local copies, waits for them, and re-layouts  12.2 us
    pallas_call x1, Pallas kernels, logit_call(): pl.pallas_call(logit_kernel, out_shape=(jax.ShapeDtypeStruct((SHARE, TOTA...  10.6 us
  transfers between devices with their start and end apart: 19, of which 3 were waited for; matrix products, arithmetic and copies ran while one was open for 4% of the time, Pallas kernels for 27%

profile of v1, /device:TPU:0, one launch (start us, length us, event | category | flops | bytes accessed | tf_op | source)
XLA Modules:
  0.0 175.3 jit_solution(6136369053666040187)
XLA Ops:
  0.7 1.2 copy.13
  2.7 2.1 %collective-permute-start.1 = (bf16[256,704]{1,0:T(8,128)(2,1)S(1)}, bf16[256,704]{1,0:T(8,128)(2,1)S(1)}, u32[]{:S(2)}, u32[]{:S(2)}) collective-permute-start(bf16[256,704]{1,0:T(8,128)(2,1)S(1)} %pad_maximum_fusion.2.refs_0_), channel_id=1, source_target_pairs={{0,64},{64,0},{1,65},{65,1},{2,66},{66,2},{3,67},{67,3},{4,68},{68... | collective-permute-start | bytes 1081352 | tf_op jit(solution)/shard_map/ppermute | solution.py:248
  4.8 1.6 collective-permute-start.2
  6.4 1.7 collective-permute-start.3
  8.0 5.9 %collective-permute-done.1.refs_2_.refs_0_ = bf16[256,704]{1,0:T(8,128)(2,1)S(1)} collective-permute-done((bf16[256,704]{1,0:T(8,128)(2,1)S(1)}, bf16[256,704]{1,0:T(8,128)(2,1)S(1)}, u32[]{:S(2)}, u32[]{:S(2)}) %collective-permute-start.1) | collective-permute-done | bytes 360480 | tf_op jit(solution)/shard_map/ppermute | solution.py:248
  14.8 1.6 collective-permute-start.7
  16.5 1.7 collective-permute-start.8
  19.2 2.0 %fusion.1 = bf16[8,272,128]{2,1,0:T(8,128)(2,1)} fusion(bf16[8,2,128]{2,1,0:T(2,128)(2,1)S(1)} %reshape.24, bf16[8,256,128]{2,1,0:T(8,128)(2,1)} %bitcast.36), kind=kLoop, calls=%fused_computation.5 | loop fusion | flops 1671168 | bytes 1085440 | tf_op jit(solution)/shard_map/concatenate | solution.py:268
  21.2 7.3 %all-to-all-start = ((bf16[8,272,128]{2,1,0:T(8,128)(2,1)}), bf16[8,272,128]{2,1,0:T(8,128)(2,1)S(1)}, u32[]{:S(2)}, u32[]{:S(2)}) async-start(bf16[8,272,128]{2,1,0:T(8,128)(2,1)} %fusion.1), calls=%async_computation | async-start | bytes 1114112 | tf_op jit(solution)/shard_map/all_to_all | solution.py:277
  28.7 2.3 %copy-done.2 = bf16[256,16,576]{0,2,1:T(8,128)(2,1)S(1)} copy-done((bf16[256,16,576]{0,2,1:T(8,128)(2,1)S(1)}, bf16[256,16,576]{0,2,1:T(8,128)(2,1)}, u32[]{:S(2)}) %copy-start.2) | copy-done | bytes 4718616
  31.0 4.8 %mass_0.1 = bf16[256,512]{1,0:T(8,128)(2,1)S(1)} custom-call(s32[17]{0:T(128)S(1)} %stack.71.ids, s32[16]{0:T(128)S(1)} %copy-done.9, bf16[16,576,256]{2,1,0:T(8,128)(2,1)S(1)} %bitcast.27, f32[16,256]{1,0:T(8,128)S(1)} %bitcast.29, bf16[256,704]{1,0:T(8,128)(2,1)S(1)} %pad_maximum_fusion.2.refs_0_, bf16[256,704]{1,0:T(8,128)(2,1)S(1)} %collective-permute-done.refs_1_), custom_call_target="tpu_custom_call" | custom-call | flops 3221225472 | bytes 5701632 | tf_op jit(solution)/shard_map/mass_0/pallas_call | solution.py:69
  36.0 2.4 %collective-permute-start.13 = (bf16[256,704]{1,0:T(8,128)(2,1)}, bf16[256,704]{1,0:T(8,128)(2,1)}, u32[]{:S(2)}, u32[]{:S(2)}) collective-permute-start(bf16[256,704]{1,0:T(8,128)(2,1)} %collective-permute-done.8.refs_9_.refs_1_), channel_id=1, source_target_pairs={{0,48},{16,0},{32,16},{48,32},{1,49},{17,1},{33,17},{49,33},{2,50}... | collective-permute-start | bytes 1081352 | tf_op jit(solution)/shard_map/ppermute | solution.py:248
  39.0 13.0 %mass_2.1 = bf16[256,1536]{1,0:T(8,128)(2,1)S(1)} custom-call(s32[17]{0:T(128)S(1)} %stack.71.ids, s32[16]{0:T(128)S(1)} %copy-done.9, bf16[16,576,256]{2,1,0:T(8,128)(2,1)} %bitcast.25, f32[16,256]{1,0:T(8,128)S(1)} %bitcast.30, bf16[256,704]{1,0:T(8,128)(2,1)S(1)} %collective-permute-done.1.refs_2_.refs_0_, ...), custom_call_target="tpu_custom_call" | custom-call | flops 9663676416 | bytes 7667712 | tf_op jit(solution)/shard_map/mass_2/pallas_call | solution.py:69
  52.0 1.1 pad_maximum_fusion
  53.3 7.2 %all-to-all-start.1 = ((bf16[8,32,2048]{2,1,0:T(8,128)(2,1)}), bf16[8,32,2048]{2,1,0:T(8,128)(2,1)S(1)}, u32[]{:S(2)}, u32[]{:S(2)}) async-start(bf16[8,32,2048]{2,1,0:T(8,128)(2,1)} %bitcast.34), calls=%async_computation.1 | async-start | bytes 2097152 | tf_op jit(solution)/shard_map/all_to_all | solution.py:285
  60.5 13.5 %mass_8.1 = bf16[256,1536]{1,0:T(8,128)(2,1)S(1)} custom-call(s32[17]{0:T(128)S(1)} %stack.71.ids, s32[16]{0:T(128)S(1)} %copy-done.9, bf16[16,576,256]{2,1,0:T(8,128)(2,1)} %bitcast.26, f32[16,256]{1,0:T(8,128)S(1)} %bitcast.31, bf16[256,704]{1,0:T(8,128)(2,1)} %collective-permute-done.7.refs_8_.refs_0_, ...), custom_call_target="tpu_custom_call" | custom-call | flops 9663676416 | bytes 7667712 | tf_op jit(solution)/shard_map/mass_8/pallas_call | solution.py:69
  74.1 2.3 %copy-done.3 = bf16[256,16,576]{0,2,1:T(8,128)(2,1)S(1)} copy-done((bf16[256,16,576]{0,2,1:T(8,128)(2,1)S(1)}, bf16[256,16,576]{0,2,1:T(8,128)(2,1)}, u32[]{:S(2)}) %copy-start.3) | copy-done | bytes 4718616
  76.4 5.9 %mass_14.1 = bf16[256,512]{1,0:T(8,128)(2,1)S(1)} custom-call(s32[17]{0:T(128)S(1)} %stack.71.ids, s32[16]{0:T(128)S(1)} %copy-done.9, bf16[16,576,256]{2,1,0:T(8,128)(2,1)S(1)} %bitcast.28, f32[16,256]{1,0:T(8,128)S(1)} %bitcast.32, bf16[256,704]{1,0:T(8,128)(2,1)} %collective-permute-done.13.refs_14_.refs_0_, ...), custom_call_target="tpu_custom_call" | custom-call | flops 3221225472 | bytes 5701632 | tf_op jit(solution)/shard_map/mass_14/pallas_call | solution.py:69
  82.3 1.1 pad_maximum_fusion.1
  83.4 7.2 %all-to-all-start.2 = ((bf16[8,32,2048]{2,1,0:T(8,128)(2,1)}), bf16[8,32,2048]{2,1,0:T(8,128)(2,1)}, u32[]{:S(2)}, u32[]{:S(2)}) async-start(bf16[8,32,2048]{2,1,0:T(8,128)(2,1)} %bitcast.33), calls=%async_computation.2 | async-start | bytes 2097152 | tf_op jit(solution)/shard_map/all_to_all | solution.py:285
  90.7 1.0 copy-done.5
  91.7 1.0 copy-done.7
  92.7 10.6 %logit.1 = (f32[32,4096]{1,0:T(8,128)}, bf16[4096,128]{1,0:T(8,128)(2,1)}, f32[8,256,128]{2,1,0:T(8,128)}) custom-call(bf16[8,272,128]{2,1,0:T(8,128)(2,1)} %copy-done, bf16[256,704]{1,0:T(8,128)(2,1)S(1)} %pad_maximum_fusion.2.refs_0_, bf16[256,704]{1,0:T(8,128)(2,1)S(1)} %collective-permute-done.refs_1_, ...), custom_call_target="tpu_custom_call" | custom-call | flops 4294967296 | bytes 4194304 | tf_op jit(solution)/shard_map/logit/pallas_call | solution.py:125
  103.3 3.2 %all-to-all-done.2.refs_1_ = bf16[8,32,2048]{2,1,0:T(8,128)(2,1)} async-done(((bf16[8,32,2048]{2,1,0:T(8,128)(2,1)}), bf16[8,32,2048]{2,1,0:T(8,128)(2,1)}, u32[]{:S(2)}, u32[]{:S(2)}) %all-to-all-start.2) | async-done | bytes 1048608 | tf_op jit(solution)/shard_map/all_to_all | solution.py:285
  106.6 1.2 copy-done.10
  107.8 1.2 copy-done.11
  109.0 1.0 copy-done.12
  110.1 26.7 %grads.1 = (bf16[8,256,128]{2,1,0:T(8,128)(2,1)S(1)}, bf16[4096,128]{1,0:T(8,128)(2,1)}) custom-call(s32[17]{0:T(128)S(1)} %stack.71.ids, s32[16]{0:T(128)S(1)} %copy-done.9, bf16[8,272,128]{2,1,0:T(8,128)(2,1)S(1)} %copy-done.1, f32[32,4096]{1,0:T(8,128)S(1)} %copy-done.12, bf16[4096,128]{1,0:T(8,128)(2,1)S(1)} %copy-done.10, ...), custom_call_target="tpu_custom_call" | custom-call | flops 12884901888 | bytes 8388608 | tf_op jit(solution)/shard_map/grads/pallas_call | solution.py:218
  136.8 14.7 %all_to_all.25 = bf16[8,256,128]{2,1,0:T(8,128)(2,1)S(1)} all-to-all(bf16[8,256,128]{2,1,0:T(8,128)(2,1)S(1)} %get-tuple-element.10), channel_id=1, replica_groups=mesh['ctx_0'=2,'ctx_1'=4,'ctx_2'=2,'head_0'=4,'head_1'=2] {'head_0','hea..., dimensions={0} | all-to-all | bytes 1048576 | tf_op jit(solution)/shard_map/all_to_all | solution.py:296
  151.5 4.6 %all-to-all-start.4 = ((bf16[128,32,128]{2,1,0:T(8,128)(2,1)}), bf16[128,32,128]{2,1,0:T(8,128)(2,1)S(1)}, u32[]{:S(2)}, u32[]{:S(2)}) async-start(bf16[128,32,128]{2,1,0:T(8,128)(2,1)} %bitcast.23), calls=%async_computation.4 | async-start | bytes 2097152 | tf_op jit(solution)/shard_map/all_to_all | solution.py:298
  156.1 1.0 convert.1
  157.2 17.3 %all-to-all-done.4 = bf16[128,32,128]{2,1,0:T(8,128)(2,1)S(1)} async-done(((bf16[128,32,128]{2,1,0:T(8,128)(2,1)}), bf16[128,32,128]{2,1,0:T(8,128)(2,1)S(1)}, u32[]{:S(2)}, u32[]{:S(2)}) %all-to-all-start.4) | async-done | bytes 1048608 | tf_op jit(solution)/shard_map/all_to_all | solution.py:298
  (53 shorter events, 4.8 us)
Async XLA Ops:
  0.6 28.0 %copy-start.9 = (s32[16]{0:T(128)S(1)}, s32[16]{0:T(128)}, u32[]{:S(2)}) copy-start(s32[16]{0:T(128)} %table.9) | copy-start | bytes 196
  0.6 28.0 %copy-start.8 = (f32[256,16]{0,1:T(8,128)S(1)}, f32[256,16]{0,1:T(8,128)}, u32[]{:S(2)}) copy-start(f32[256,16]{0,1:T(8,128)} %param.10) | copy-start | bytes 49156
  2.7 11.2 %collective-permute-start.1 = (bf16[256,704]{1,0:T(8,128)(2,1)S(1)}, bf16[256,704]{1,0:T(8,128)(2,1)S(1)}, u32[]{:S(2)}, u32[]{:S(2)}) collective-permute-start(bf16[256,704]{1,0:T(8,128)(2,1)S(1)} %pad_maximum_fusion.2.refs_0_), channel_id=1, source_target_pairs={{0,64},{64,0},{1,65},{65,1},{2,66},{66,2},{3,67},{67,3},{4,68},{68... | collective-permute-start | bytes 1081352 | tf_op jit(solution)/shard_map/ppermute | solution.py:248
  4.8 11.7 %collective-permute-start = (bf16[256,704]{1,0:T(8,128)(2,1)S(1)}, bf16[256,704]{1,0:T(8,128)(2,1)S(1)}, u32[]{:S(2)}, u32[]{:S(2)}) collective-permute-start(bf16[256,704]{1,0:T(8,128)(2,1)S(1)} %pad_maximum_fusion.2.refs_0_), channel_id=1, source_target_pairs={{0,8},{8,0},{1,9},{9,1},{2,10},{10,2},{3,11},{11,3},{4,12},{12,4},... | collective-permute-start | bytes 1081352 | tf_op jit(solution)/shard_map/ppermute | solution.py:248
  4.8 13.4 %collective-permute-start.2 = (bf16[256,704]{1,0:T(8,128)(2,1)S(1)}, bf16[256,704]{1,0:T(8,128)(2,1)S(1)}, u32[]{:S(2)}, u32[]{:S(2)}) collective-permute-start(bf16[256,704]{1,0:T(8,128)(2,1)S(1)} %pad_maximum_fusion.2.refs_0_), channel_id=1, source_target_pairs={{0,16},{16,32},{32,48},{48,0},{1,17},{17,33},{33,49},{49,1},{2,18}... | collective-permute-start | bytes 1081352 | tf_op jit(solution)/shard_map/ppermute | solution.py:248
  6.4 11.9 %collective-permute-start.3 = (bf16[256,704]{1,0:T(8,128)(2,1)S(1)}, bf16[256,704]{1,0:T(8,128)(2,1)S(1)}, u32[]{:S(2)}, u32[]{:S(2)}) collective-permute-start(bf16[256,704]{1,0:T(8,128)(2,1)S(1)} %pad_maximum_fusion.2.refs_0_), channel_id=1, source_target_pairs={{0,48},{16,0},{32,16},{48,32},{1,49},{17,1},{33,17},{49,33},{2,50}... | collective-permute-start | bytes 1081352 | tf_op jit(solution)/shard_map/ppermute | solution.py:248
  13.9 5.3 %collective-permute-start.4 = (bf16[256,704]{1,0:T(8,128)(2,1)S(1)}, bf16[256,704]{1,0:T(8,128)(2,1)S(1)}, u32[]{:S(2)}, u32[]{:S(2)}) collective-permute-start(bf16[256,704]{1,0:T(8,128)(2,1)S(1)} %collective-permute-done.1.refs_2_.refs_0_), channel_id=1, source_target_pairs={{0,8},{8,0},{1,9},{9,1},{2,10},{10,2},{3,11},{11,3},{4,12},{12,4},... | collective-permute-start | bytes 1081352 | tf_op jit(solution)/shard_map/ppermute | solution.py:248
  14.8 23.6 %collective-permute-start.7 = (bf16[256,704]{1,0:T(8,128)(2,1)S(1)}, bf16[256,704]{1,0:T(8,128)(2,1)}, u32[]{:S(2)}, u32[]{:S(2)}) collective-permute-start(bf16[256,704]{1,0:T(8,128)(2,1)S(1)} %collective-permute-done.1.refs_2_.refs_0_), channel_id=1, source_target_pairs={{0,16},{16,32},{32,48},{48,0},{1,17},{17,33},{33,49},{49,1},{2,18}... | collective-permute-start | bytes 1081352 | tf_op jit(solution)/shard_map/ppermute | solution.py:248
  16.5 19.4 %collective-permute-start.8 = (bf16[256,704]{1,0:T(8,128)(2,1)S(1)}, bf16[256,704]{1,0:T(8,128)(2,1)}, u32[]{:S(2)}, u32[]{:S(2)}) collective-permute-start(bf16[256,704]{1,0:T(8,128)(2,1)S(1)} %collective-permute-done.1.refs_2_.refs_0_), channel_id=1, source_target_pairs={{0,48},{16,0},{32,16},{48,32},{1,49},{17,1},{33,17},{49,33},{2,50}... | collective-permute-start | bytes 1081352 | tf_op jit(solution)/shard_map/ppermute | solution.py:248
  18.2 17.8 %collective-permute-start.5 = (bf16[256,704]{1,0:T(8,128)(2,1)S(1)}, bf16[256,704]{1,0:T(8,128)(2,1)}, u32[]{:S(2)}, u32[]{:S(2)}) collective-permute-start(bf16[256,704]{1,0:T(8,128)(2,1)S(1)} %collective-permute-done.2.refs_3_.refs_1_), channel_id=1, source_target_pairs={{0,8},{8,0},{1,9},{9,1},{2,10},{10,2},{3,11},{11,3},{4,12},{12,4},... | collective-permute-start | bytes 1081352 | tf_op jit(solution)/shard_map/ppermute | solution.py:248
  18.2 20.7 %copy-start.4 = (bf16[256,704]{1,0:T(8,128)(2,1)}, bf16[256,704]{1,0:T(8,128)(2,1)S(1)}, u32[]{:S(2)}) copy-start(bf16[256,704]{1,0:T(8,128)(2,1)S(1)} %collective-permute-done.3.refs_4_.refs_2_) | copy-start | bytes 1081348
  18.3 20.3 %collective-permute-start.9 = (bf16[256,704]{1,0:T(8,128)(2,1)S(1)}, bf16[256,704]{1,0:T(8,128)(2,1)}, u32[]{:S(2)}, u32[]{:S(2)}) collective-permute-start(bf16[256,704]{1,0:T(8,128)(2,1)S(1)} %collective-permute-done.2.refs_3_.refs_1_), channel_id=1, source_target_pairs={{0,16},{16,32},{32,48},{48,0},{1,17},{17,33},{33,49},{49,1},{2,18}... | collective-permute-start | bytes 1081352 | tf_op jit(solution)/shard_map/ppermute | solution.py:248
  19.2 19.7 %copy-start.6 = (bf16[256,704]{1,0:T(8,128)(2,1)}, bf16[256,704]{1,0:T(8,128)(2,1)S(1)}, u32[]{:S(2)}) copy-start(bf16[256,704]{1,0:T(8,128)(2,1)S(1)} %collective-permute-done.4.refs_5_.refs_3_) | copy-start | bytes 1081348
  19.2 19.7 %collective-permute-start.6 = (bf16[256,704]{1,0:T(8,128)(2,1)S(1)}, bf16[256,704]{1,0:T(8,128)(2,1)}, u32[]{:S(2)}, u32[]{:S(2)}) collective-permute-start(bf16[256,704]{1,0:T(8,128)(2,1)S(1)} %collective-permute-done.3.refs_4_.refs_2_), channel_id=1, source_target_pairs={{0,8},{8,0},{1,9},{9,1},{2,10},{10,2},{3,11},{11,3},{4,12},{12,4},... | collective-permute-start | bytes 1081352 | tf_op jit(solution)/shard_map/ppermute | solution.py:248
  21.2 32.0 %all-to-all-start = ((bf16[8,272,128]{2,1,0:T(8,128)(2,1)}), bf16[8,272,128]{2,1,0:T(8,128)(2,1)S(1)}, u32[]{:S(2)}, u32[]{:S(2)}) async-start(bf16[8,272,128]{2,1,0:T(8,128)(2,1)} %fusion.1), calls=%async_computation | async-start | bytes 1114112 | tf_op jit(solution)/shard_map/all_to_all | solution.py:277
  28.7 2.3 %copy-start.2 = (bf16[256,16,576]{0,2,1:T(8,128)(2,1)S(1)}, bf16[256,16,576]{0,2,1:T(8,128)(2,1)}, u32[]{:S(2)}) copy-start(bf16[256,16,576]{0,2,1:T(8,128)(2,1)} %param.8) | copy-start | bytes 14155780
  35.8 24.6 %collective-permute-start.11 = (bf16[256,704]{1,0:T(8,128)(2,1)}, bf16[256,704]{1,0:T(8,128)(2,1)}, u32[]{:S(2)}, u32[]{:S(2)}) collective-permute-start(bf16[256,704]{1,0:T(8,128)(2,1)} %collective-permute-done.8.refs_9_.refs_1_), channel_id=1, source_target_pairs={{0,8},{8,0},{1,9},{9,1},{2,10},{10,2},{3,11},{11,3},{4,12},{12,4},... | collective-permute-start | bytes 1081352 | tf_op jit(solution)/shard_map/ppermute | solution.py:248
  36.0 17.1 %collective-permute-start.13 = (bf16[256,704]{1,0:T(8,128)(2,1)}, bf16[256,704]{1,0:T(8,128)(2,1)}, u32[]{:S(2)}, u32[]{:S(2)}) collective-permute-start(bf16[256,704]{1,0:T(8,128)(2,1)} %collective-permute-done.8.refs_9_.refs_1_), channel_id=1, source_target_pairs={{0,48},{16,0},{32,16},{48,32},{1,49},{17,1},{33,17},{49,33},{2,50}... | collective-permute-start | bytes 1081352 | tf_op jit(solution)/shard_map/ppermute | solution.py:248
  38.4 22.1 %collective-permute-start.10 = (bf16[256,704]{1,0:T(8,128)(2,1)}, bf16[256,704]{1,0:T(8,128)(2,1)}, u32[]{:S(2)}, u32[]{:S(2)}) collective-permute-start(bf16[256,704]{1,0:T(8,128)(2,1)} %collective-permute-done.7.refs_8_.refs_0_), channel_id=1, source_target_pairs={{0,8},{8,0},{1,9},{9,1},{2,10},{10,2},{3,11},{11,3},{4,12},{12,4},... | collective-permute-start | bytes 1081352 | tf_op jit(solution)/shard_map/ppermute | solution.py:248
  38.6 21.9 %collective-permute-start.12 = (bf16[256,704]{1,0:T(8,128)(2,1)}, bf16[256,704]{1,0:T(8,128)(2,1)}, u32[]{:S(2)}, u32[]{:S(2)}) collective-permute-start(bf16[256,704]{1,0:T(8,128)(2,1)} %collective-permute-done.9.refs_10_.refs_2_), channel_id=1, source_target_pairs={{0,8},{8,0},{1,9},{9,1},{2,10},{10,2},{3,11},{11,3},{4,12},{12,4},... | collective-permute-start | bytes 1081352 | tf_op jit(solution)/shard_map/ppermute | solution.py:248
  53.1 20.9 %collective-permute-start.14 = (bf16[256,704]{1,0:T(8,128)(2,1)}, bf16[256,704]{1,0:T(8,128)(2,1)}, u32[]{:S(2)}, u32[]{:S(2)}) collective-permute-start(bf16[256,704]{1,0:T(8,128)(2,1)} %collective-permute-done.13.refs_14_.refs_0_), channel_id=1, source_target_pairs={{0,8},{8,0},{1,9},{9,1},{2,10},{10,2},{3,11},{11,3},{4,12},{12,4},... | collective-permute-start | bytes 1081352 | tf_op jit(solution)/shard_map/ppermute | solution.py:248
  53.3 20.8 %copy-start = (bf16[8,272,128]{2,1,0:T(8,128)(2,1)}, bf16[8,272,128]{2,1,0:T(8,128)(2,1)S(1)}, u32[]{:S(2)}) copy-start(bf16[8,272,128]{2,1,0:T(8,128)(2,1)S(1)} %all-to-all-done.qw_ref) | copy-start | bytes 1671172
  53.3 30.2 %all-to-all-start.1 = ((bf16[8,32,2048]{2,1,0:T(8,128)(2,1)}), bf16[8,32,2048]{2,1,0:T(8,128)(2,1)S(1)}, u32[]{:S(2)}, u32[]{:S(2)}) async-start(bf16[8,32,2048]{2,1,0:T(8,128)(2,1)} %bitcast.34), calls=%async_computation.1 | async-start | bytes 2097152 | tf_op jit(solution)/shard_map/all_to_all | solution.py:285
  74.1 2.3 %copy-start.3 = (bf16[256,16,576]{0,2,1:T(8,128)(2,1)S(1)}, bf16[256,16,576]{0,2,1:T(8,128)(2,1)}, u32[]{:S(2)}) copy-start(bf16[256,16,576]{0,2,1:T(8,128)(2,1)} %param.8) | copy-start | bytes 14155780
  82.3 8.3 %copy-start.13 = (f32[256]{0:T(256)S(1)}, f32[256]{0:T(256)}, u32[]{:S(2)}) copy-start(f32[256]{0:T(256)} %param.14) | copy-start | bytes 3076
  83.4 23.1 %all-to-all-start.2 = ((bf16[8,32,2048]{2,1,0:T(8,128)(2,1)}), bf16[8,32,2048]{2,1,0:T(8,128)(2,1)}, u32[]{:S(2)}, u32[]{:S(2)}) async-start(bf16[8,32,2048]{2,1,0:T(8,128)(2,1)} %bitcast.33), calls=%async_computation.2 | async-start | bytes 2097152 | tf_op jit(solution)/shard_map/all_to_all | solution.py:285
  90.7 1.0 copy-start.5
  92.7 13.9 %copy-start.1 = (bf16[8,272,128]{2,1,0:T(8,128)(2,1)S(1)}, bf16[8,272,128]{2,1,0:T(8,128)(2,1)}, u32[]{:S(2)}) copy-start(bf16[8,272,128]{2,1,0:T(8,128)(2,1)} %copy-done) | copy-start | bytes 1671172
  106.6 1.2 copy-start.10
  107.8 1.2 copy-start.11
  109.0 1.0 copy-start.12
  151.5 23.0 %all-to-all-start.4 = ((bf16[128,32,128]{2,1,0:T(8,128)(2,1)}), bf16[128,32,128]{2,1,0:T(8,128)(2,1)S(1)}, u32[]{:S(2)}, u32[]{:S(2)}) async-start(bf16[128,32,128]{2,1,0:T(8,128)(2,1)} %bitcast.23), calls=%async_computation.4 | async-start | bytes 2097152 | tf_op jit(solution)/shard_map/all_to_all | solution.py:298
  (1 other events, 1.0 us)

commit v2 on v1

v2 whole, which is shorter than its diff:
```python
import functools

import jax
import jax.numpy as jnp
from jax import lax
from jax.experimental import pallas as pl
from jax.experimental.pallas import tpu as pltpu
from jax.sharding import Mesh
from jax.sharding import PartitionSpec as P

CTX = ("ctx_0", "ctx_1", "ctx_2")
HEAD = ("head_0", "head_1")
ALL = CTX + HEAD

ROWS = 256
LATENT = 576
IDIM = 128
HEADS_DEV = 16
PEERS = 8
SHARE = ROWS // PEERS
BLOCKS = 16
TOTAL = BLOCKS * ROWS
PAD = 16
LOG2E = 1.4426950408889634
SCORE = 192.0 ** -0.5
ISCALE = IDIM ** -0.5
WIDE = 1024
MIB = 2**20

ORDER = (
    (0, 0, 0), (0, 0, 1),
    (1, 0, 0), (0, 3, 0), (0, 1, 0), (1, 0, 1), (0, 3, 1), (0, 1, 1),
    (1, 3, 0), (1, 1, 0), (0, 2, 0), (1, 3, 1), (1, 1, 1), (0, 2, 1), (1, 2, 0), (1, 2, 1),
)

SORTED = tuple(k for p in range(2) for k in range(BLOCKS) if ORDER[k][2] == p)
PLACE = tuple(SORTED.index(k) for k in range(BLOCKS))
HALF = TOTAL // 2
VMEM = pltpu.VMEM


def mass_kernel(first, count, carried, hstep, ids, table, q_ref, lse_ref, *refs):
    blocks, extra = refs[:count], refs[count : count + carried]
    out_ref, keys_ref, acc = refs[count + carried :]
    step = pl.program_id(0)

    @pl.when(step == 0)
    def _():
        acc[...] = jnp.zeros_like(acc)
        for b in range(count):
            keys_ref[b * ROWS : (b + 1) * ROWS, :] = blocks[b][:, :IDIM]

    for b in range(count):
        lat = blocks[b][:, IDIM : IDIM + LATENT]
        rows = slice(b * ROWS, (b + 1) * ROWS)
        part = None
        for i in range(hstep):
            s = jnp.dot(lat, q_ref[step * hstep + i], preferred_element_type=jnp.float32)
            lse = lse_ref[pl.ds(step * hstep + i, 1), :] * jnp.float32(LOG2E)
            e = jnp.exp2(s * jnp.float32(SCORE * LOG2E) - lse)
            part = e if part is None else part + e
        acc[rows, :] += part

    @pl.when(step == pl.num_programs(0) - 1)
    def _():
        place = 0
        for ref in extra:
            size = ref.shape[1]
            out_ref[:, place : place + size, :] = ref[...]
            place += size
        q_pos = table[ids[0]] + lax.broadcasted_iota(jnp.int32, (ROWS, ROWS), 0)
        for b in range(count):
            k_pos = table[ids[first + b]] + lax.broadcasted_iota(jnp.int32, (ROWS, ROWS), 1)
            mass = acc[b * ROWS : (b + 1) * ROWS, :].T
            mass = jnp.where(k_pos <= q_pos, mass, jnp.float32(0.0)).astype(jnp.bfloat16)
            for i in range(2):
                half = mass[:, i * IDIM : (i + 1) * IDIM].reshape(PEERS, SHARE, IDIM)
                out_ref[:, place : place + SHARE, :] = half
                place += SHARE


def mass_call(ids, table, q_t, lse_t, blocks, first, extra=(), hstep=4):
    count = len(blocks)
    width = blocks[0].shape[1]
    rows = sum(e.shape[1] for e in extra) + count * 2 * SHARE
    return pl.pallas_call(
        functools.partial(mass_kernel, first, count, len(extra), hstep),
        out_shape=(
            jax.ShapeDtypeStruct((PEERS, rows, IDIM), jnp.bfloat16),
            jax.ShapeDtypeStruct((count * ROWS, IDIM), jnp.bfloat16),
        ),
        grid_spec=pltpu.PrefetchScalarGridSpec(
            num_scalar_prefetch=2,
            grid=(HEADS_DEV // hstep,),
            in_specs=[
                pl.BlockSpec(memory_space=VMEM),
                pl.BlockSpec((HEADS_DEV, ROWS), lambda h, *_: (0, 0)),
            ]
            + [pl.BlockSpec((ROWS, width), lambda h, *_: (0, 0))] * count
            + [pl.BlockSpec(e.shape, lambda h, *_: (0, 0, 0)) for e in extra],
            out_specs=(
                pl.BlockSpec((PEERS, rows, IDIM), lambda h, *_: (0, 0, 0)),
                pl.BlockSpec((count * ROWS, IDIM), lambda h, *_: (0, 0)),
            ),
            scratch_shapes=[pltpu.VMEM((count * ROWS, ROWS), jnp.float32)],
        ),
        compiler_params=pltpu.CompilerParams(vmem_limit_bytes=24 * MIB),
        cost_estimate=pl.CostEstimate(
            flops=2 * HEADS_DEV * ROWS * ROWS * count * LATENT * 4 // 3,
            bytes_accessed=HEADS_DEV * ROWS * LATENT * 2 + count * ROWS * (width + ROWS) * 2,
            transcendentals=HEADS_DEV * ROWS * ROWS * count,
        ),
        name="mass_%d" % first,
    )(ids, table, q_t, lse_t, *blocks, *extra)


def prob_kernel(ids, table, loss_ref, qw_ref, *refs):
    pieces = refs[:-5]
    prob_ref, keys_ref, gates_ref, wide, logit = refs[-5:]
    step = pl.program_id(0)

    @pl.when(step == 0)
    def _():
        done = 0
        for piece in pieces:
            for start in range(0, piece.shape[0], ROWS):
                place = PLACE[done] * ROWS
                keys_ref[place : place + ROWS, :] = piece[start : start + ROWS, :]
                done += 1
        for h in range(PEERS):
            w = qw_ref[h, ROWS : ROWS + PAD, :].astype(jnp.float32)
            for i in range(2):
                wide[h, i * IDIM : (i + 1) * IDIM, :] = jnp.broadcast_to(
                    w[i : i + 1, :], (IDIM, IDIM)
                ).T

    count = WIDE // IDIM
    start = pl.multiple_of(step * WIDE, WIDE)
    keys = keys_ref[pl.ds(start, WIDE), :]
    acc = [None] * count
    for h in range(PEERS):
        dots = lax.dot_general(
            qw_ref[h, :ROWS, :], keys, (((1,), (1,)), ((), ())),
            preferred_element_type=jnp.float32,
        )
        w = wide[h]
        rows = slice(h * ROWS, (h + 1) * ROWS)
        for i in range(count):
            cols = slice(i * IDIM, (i + 1) * IDIM)
            gate = jnp.where(dots[:, cols] > 0, w, jnp.float32(0.0))
            gates_ref[rows, cols] = gate.astype(jnp.bfloat16)
            y = gate * dots[:, cols]
            acc[i] = y if acc[i] is None else acc[i] + y
    for i in range(count):
        cols = pl.ds(pl.multiple_of(start + i * IDIM, IDIM), IDIM)
        logit[:, cols] = jnp.sum(acc[i].reshape(SHARE, PEERS, IDIM), axis=1)

    @pl.when(step == pl.num_programs(0) - 1)
    def _():
        sub = ids[BLOCKS] * SHARE
        q_pos = table[ids[0]] + sub + lax.broadcasted_iota(jnp.int32, (SHARE, ROWS), 0)
        lane = lax.broadcasted_iota(jnp.int32, (SHARE, ROWS), 1)
        peak = None
        for b in range(BLOCKS):
            cols = slice(b * ROWS, (b + 1) * ROWS)
            masked = jnp.where(
                table[ids[SORTED[b]]] + lane <= q_pos,
                logit[:, cols] * jnp.float32(ISCALE),
                jnp.float32(-1e30),
            )
            logit[:, cols] = masked
            peak = masked if peak is None else jnp.maximum(peak, masked)
        peak = jnp.max(peak, axis=1, keepdims=True)
        total = None
        for b in range(BLOCKS):
            cols = slice(b * ROWS, (b + 1) * ROWS)
            e = jnp.exp(logit[:, cols] - peak)
            logit[:, cols] = e
            total = e if total is None else total + e
        total = loss_ref[:, :1] / jnp.sum(total, axis=1, keepdims=True)
        for b in range(BLOCKS):
            cols = slice(b * ROWS, (b + 1) * ROWS)
            prob_ref[:, cols] = logit[:, cols] * total


def prob_call(ids, table, loss, qw, pieces):
    return pl.pallas_call(
        prob_kernel,
        out_shape=(
            jax.ShapeDtypeStruct((SHARE, TOTAL), jnp.float32),
            jax.ShapeDtypeStruct((TOTAL, IDIM), jnp.bfloat16),
            jax.ShapeDtypeStruct((PEERS * ROWS, TOTAL), jnp.bfloat16),
        ),
        grid_spec=pltpu.PrefetchScalarGridSpec(
            num_scalar_prefetch=2,
            grid=(TOTAL // WIDE,),
            in_specs=[
                pl.BlockSpec((SHARE, IDIM), lambda i, *_: (0, 0)),
                pl.BlockSpec((PEERS, ROWS + PAD, IDIM), lambda i, *_: (0, 0, 0)),
            ]
            + [pl.BlockSpec(p.shape, lambda i, *_: (0, 0)) for p in pieces],
            out_specs=(
                pl.BlockSpec((SHARE, TOTAL), lambda i, *_: (0, 0)),
                pl.BlockSpec((TOTAL, IDIM), lambda i, *_: (0, 0)),
                pl.BlockSpec((PEERS * ROWS, WIDE), lambda i, *_: (0, i)),
            ),
            scratch_shapes=[
                pltpu.VMEM((PEERS, ROWS, IDIM), jnp.float32),
                pltpu.VMEM((SHARE, TOTAL), jnp.float32),
            ],
        ),
        compiler_params=pltpu.CompilerParams(vmem_limit_bytes=60 * MIB),
        cost_estimate=pl.CostEstimate(
            flops=8 * PEERS * ROWS * TOTAL * IDIM, bytes_accessed=20 * MIB, transcendentals=0
        ),
        name="probs",
    )(ids, table, loss, qw, *pieces)


def coef_tile(coefs, g, gates_ref):
    g = jnp.broadcast_to(g[:, None, :], (SHARE, PEERS, WIDE)).reshape(ROWS, WIDE)
    for h in range(PEERS):
        part = slice(h * ROWS, (h + 1) * ROWS)
        coefs[part, :] = (g * gates_ref[part, :].astype(jnp.float32)).astype(jnp.bfloat16)


def kterm_tile(coefs, q_t):
    kterm = jnp.dot(q_t[...], coefs[...], preferred_element_type=jnp.float32)
    return (kterm * jnp.float32(ISCALE)).T


def grad_kernel(starts, ids, prob_ref, keys_ref, gates_ref, loss_ref, *refs):
    raws = refs[: len(starts)]
    qgrad_ref, kterm_ref, half_ref, q_t, grad, acc, coefs = refs[len(starts) :]
    qw_ref = raws[0]
    step = pl.program_id(0)

    @pl.when(step == 0)
    def _():
        mass = None
        done = 0
        for ref, start in zip(raws, starts):
            for place in range(start, ref.shape[1], SHARE):
                part = ref[0, place : place + SHARE, :].astype(jnp.float32)
                for p in range(1, PEERS):
                    part = part + ref[p, place : place + SHARE, :].astype(jnp.float32)
                col = (PLACE[done // 2] * 2 + done % 2) * IDIM
                grad[:, col : col + IDIM] = part
                mass = part if mass is None else mass + part
                done += 1
        mass = loss_ref[:, :1] / jnp.sum(mass, axis=1, keepdims=True)
        for b in range(BLOCKS):
            cols = slice(b * ROWS, (b + 1) * ROWS)
            grad[:, cols] = prob_ref[:, cols] - grad[:, cols] * mass
        half_ref[...] = grad[:, :HALF]
        for h in range(PEERS):
            q_t[:, h * ROWS : (h + 1) * ROWS] = qw_ref[h, :ROWS, :].T
        acc[...] = jnp.zeros_like(acc)

    rows = pl.ds(pl.multiple_of(step * WIDE, WIDE), WIDE)
    coef_tile(coefs, grad[:, rows], gates_ref)
    acc[...] += jnp.dot(coefs[...], keys_ref[rows, :], preferred_element_type=jnp.float32)
    for tile in range(HALF // WIDE, TOTAL // WIDE):

        @pl.when(step == tile)
        def _():
            kterm = kterm_tile(coefs, q_t)
            for i in range(WIDE // ROWS):
                place = ids[SORTED[tile * (WIDE // ROWS) + i]] >> 1
                place = pl.ds(pl.multiple_of(place * ROWS, ROWS), ROWS)
                kterm_ref[place, :] = kterm[i * ROWS : (i + 1) * ROWS, :]

    @pl.when(step == pl.num_programs(0) - 1)
    def _():
        for h in range(PEERS):
            qgrad = acc[h * ROWS : (h + 1) * ROWS, :] * jnp.float32(ISCALE)
            qgrad_ref[h] = qgrad.astype(jnp.bfloat16)


def whole(a):
    return pl.BlockSpec(a.shape, lambda i, *_: (0,) * len(a.shape))


GATES = pl.BlockSpec((PEERS * ROWS, WIDE), lambda i, *_: (0, i))


def grad_call(ids, prob, keys, gates, loss, raws, starts):
    out_shape = (
        jax.ShapeDtypeStruct((PEERS, ROWS, IDIM), jnp.bfloat16),
        jax.ShapeDtypeStruct((HALF, IDIM), jnp.float32),
        jax.ShapeDtypeStruct((SHARE, HALF), jnp.float32),
        jax.ShapeDtypeStruct((IDIM, PEERS * ROWS), jnp.bfloat16),
    )
    return pl.pallas_call(
        functools.partial(grad_kernel, starts),
        out_shape=out_shape,
        grid_spec=pltpu.PrefetchScalarGridSpec(
            num_scalar_prefetch=1,
            grid=(TOTAL // WIDE,),
            in_specs=[whole(prob), whole(keys), GATES, whole(loss)] + [whole(r) for r in raws],
            out_specs=tuple(whole(o) for o in out_shape),
            scratch_shapes=[
                pltpu.VMEM((SHARE, TOTAL), jnp.float32),
                pltpu.VMEM((PEERS * ROWS, IDIM), jnp.float32),
                pltpu.VMEM((PEERS * ROWS, WIDE), jnp.bfloat16),
            ],
        ),
        compiler_params=pltpu.CompilerParams(vmem_limit_bytes=60 * MIB),
        cost_estimate=pl.CostEstimate(
            flops=6 * PEERS * ROWS * TOTAL * IDIM, bytes_accessed=26 * MIB, transcendentals=0
        ),
        name="grads",
    )(ids, prob, keys, gates, loss, *raws)


def kterm_kernel(ids, half_ref, gates_ref, q_t, other_ref, out_ref, coefs):
    step = pl.program_id(0)
    for tile in range(HALF // WIDE):

        @pl.when(step == tile)
        def _():
            coef_tile(coefs, half_ref[:, tile * WIDE : (tile + 1) * WIDE], gates_ref)
            kterm = kterm_tile(coefs, q_t)
            for i in range(WIDE // ROWS):
                place = ids[SORTED[tile * (WIDE // ROWS) + i]] >> 1
                place = pl.ds(pl.multiple_of(place * ROWS, ROWS), ROWS)
                part = kterm[i * ROWS : (i + 1) * ROWS, :] + other_ref[place, :]
                out_ref[place, :] = part.astype(jnp.bfloat16)


def kterm_call(ids, half, gates, q_t, other):
    out = jax.ShapeDtypeStruct((HALF, IDIM), jnp.bfloat16)
    return pl.pallas_call(
        kterm_kernel,
        out_shape=out,
        grid_spec=pltpu.PrefetchScalarGridSpec(
            num_scalar_prefetch=1,
            grid=(HALF // WIDE,),
            in_specs=[whole(half), GATES, whole(q_t), whole(other)],
            out_specs=whole(out),
            scratch_shapes=[pltpu.VMEM((PEERS * ROWS, WIDE), jnp.bfloat16)],
        ),
        compiler_params=pltpu.CompilerParams(vmem_limit_bytes=60 * MIB),
        cost_estimate=pl.CostEstimate(
            flops=2 * PEERS * ROWS * TOTAL * IDIM, bytes_accessed=12 * MIB, transcendentals=0
        ),
        name="kterms",
    )(ids, half, gates, q_t, other)


def shift(array, axis, size, by):
    return lax.ppermute(array, axis, [(i, (i + by) % size) for i in range(size)])


def local(
    main_queries, latents, saved_lse, index_queries, index_keys, head_weights, row_weight,
    block_offsets,
):
    c0, c1, c2 = (lax.axis_index(a) for a in CTX)
    head = lax.axis_index(HEAD)
    ids = [(c0 ^ a) * 8 + ((c1 + b) & 3) * 2 + (c2 ^ c) for a, b, c in ORDER]
    ids = jnp.stack([i.astype(jnp.int32) for i in ids + [head]])

    own = jnp.concatenate([index_keys, latents], axis=1)
    core = functools.partial(shift, axis="ctx_2", size=2, by=1)
    up = functools.partial(shift, axis="ctx_1", size=4, by=1)
    down = functools.partial(shift, axis="ctx_1", size=4, by=-1)
    side = functools.partial(shift, axis="ctx_0", size=2, by=1)

    weights = head_weights.reshape(PEERS, 2, IDIM)
    weights = jnp.pad(weights, ((0, 0), (0, PAD - 2), (0, 0)))
    qw = jnp.concatenate([index_queries.reshape(PEERS, ROWS, IDIM), weights], axis=1)

    q_t = jnp.transpose(main_queries, (1, 2, 0))
    lse_t = saved_lse.T
    loss = lax.dynamic_slice_in_dim(row_weight, head * SHARE, SHARE, 0)
    loss = jnp.broadcast_to(loss[:, None], (SHARE, IDIM))
    q_t, lse_t, loss, qw, ids = lax.optimization_barrier((q_t, lse_t, loss, qw, ids))
    mass = functools.partial(mass_call, ids, block_offsets, q_t, lse_t)

    q_t = jnp.transpose(main_queries, (1, 2, 0))
    lse_t = saved_lse.T
    loss = lax.dynamic_slice_in_dim(row_weight, head * SHARE, SHARE, 0)
    loss = jnp.broadcast_to(loss[:, None], (SHARE, IDIM))
    q_t, lse_t, loss, qw, ids = lax.optimization_barrier((q_t, lse_t, loss, qw, ids))
    mass = functools.partial(mass_call, ids, block_offsets, q_t, lse_t)

    pair = core(own)
    z, yp, ym = side(own), up(own), down(own)
    near, keys_0 = mass([own, pair], 0)
    z, yp, ym, near = lax.optimization_barrier((z, yp, ym, near))
    zyp, zym, y2 = up(z), down(z), up(yp)
    pz, pyp, pym = core(z), core(yp), core(ym)
    raw_0, keys_1 = mass([z, yp, ym, pz, pyp, pym], 2, (qw, near))
    zyp, zym, y2, raw_0 = lax.optimization_barrier((zyp, zym, y2, raw_0))
    pzyp, pzym, py2 = core(zyp), core(zym), core(y2)
    zy2, pzy2 = down(zym), up(pzyp)
    raw_0 = lax.all_to_all(raw_0, HEAD, 0, 0, tiled=True)
    raw_1, keys_2 = mass([zyp, zym, y2, pzyp, pzym, py2, zy2, pzy2], 8)
    raw_1 = lax.all_to_all(raw_1, HEAD, 0, 0, tiled=True)

    prob, keys, gates = prob_call(ids, block_offsets, loss, raw_0, (keys_0, keys_1, keys_2))
    qgrad, other, half, i_t = grad_call(
        ids, prob, keys, gates, loss, (raw_0, raw_1), (ROWS + PAD, 0)
    )
    other = core(other)
    qgrad = lax.all_to_all(qgrad, HEAD, 0, 0, tiled=True)
    kterm = kterm_call(ids, half, gates, i_t, other)
    kterm = kterm.reshape(HALF // SHARE, SHARE, IDIM)
    kterm = lax.all_to_all(kterm, CTX[:2] + HEAD, 0, 0, tiled=True)
    query_grads = qgrad.reshape(ROWS, PEERS, IDIM).astype(jnp.float32)
    key_grads = jnp.sum(kterm.astype(jnp.float32), axis=0)
    return query_grads, key_grads


def solution(mesh):
    torus = Mesh(mesh.devices.reshape(2, 4, 2, 4, 2), ALL)
    placed = (
        P(CTX, HEAD, None), P(CTX, None), P(CTX, HEAD), P(CTX, HEAD, None), P(CTX, None),
        P(CTX, HEAD), P(CTX), P(),
    )
    return jax.shard_map(
        local,
        mesh=torus,
        in_specs=placed,
        out_specs=(P(CTX, HEAD, None), P(ALL, None)),
        check_vma=False,
    )
```

time: 176 us -> 147 us (0.84)
  blocking collectives: 14.7 us -> 0 us
  Pallas kernels: 74.5 us -> 67.8 us
  starting transfers between devices: 39.3 us -> 34.5 us
  other arithmetic: 6.96 us -> 2.68 us
  waiting for transfers between devices: 26.4 us -> 30.3 us
  local copies, waits for them, and re-layouts: 12.5 us -> 10.5 us
    all_to_all x1 -> x0, blocking collectives: 14.7 us -> none  [local(): qgrad = lax.all_to_all(qgrad, HEAD, 0, 0, tiled=True)]
    pallas_call x6, Pallas kernels: 74.5 us -> 67.8 us  [the longest x3 33.8 us: mass_call(): pl.pallas_call(functools.partial(mass_kernel, first, count, len(extra), h...]
    ppermute x15 -> x16, waiting for transfers between devices: 5.91 us -> 10.8 us  [shift(): lax.ppermute(array, axis, [(i, (i + by) % size) for i in range(size)])]
    all_to_all x4, starting transfers between devices: 26.4 us -> 23.5 us  [the longest x1 7.61 us: local(): raw_0 = lax.all_to_all(raw_0, HEAD, 0, 0, tiled=True)]
    unnamed x30 -> x28, local copies, waits for them, and re-layouts: 12.2 us -> 9.53 us
    concatenate x2 -> x0, other arithmetic: 2.2 us -> none  [exchange(): m = jnp.concatenate(parts, axis=1).reshape(PEERS, SHARE, -1)]
    concatenate x1, other arithmetic: 2.03 us -> 0.04 us  [local(): jnp.concatenate([index_queries.reshape(PEERS, ROWS, IDIM), weights], axis=1)]
    ppermute x15 -> x16, starting transfers between devices: 12.9 us -> 11 us  [shift(): lax.ppermute(array, axis, [(i, (i + by) % size) for i in range(size)])]
  transfers between devices with their start and end apart: 19 -> 20, of which waited for: 3 -> 9; matrix products, arithmetic and copies ran while one was open for 4% -> 1% of each run, Pallas kernels for 27% -> 37%
where the time goes in v2:
time: 147 us
  Pallas kernels  67.8 us (46%)
  starting transfers between devices  34.5 us (23%)
  waiting for transfers between devices  30.3 us (21%)
  local copies, waits for them, and re-layouts  10.5 us (7%)
  other arithmetic  2.68 us (2%)
    pallas_call x3, Pallas kernels, mass_call(): pl.pallas_call(functools.partial(mass_kernel, first, count, len(extra), h...  33.8 us
    pallas_call x1, Pallas kernels, grad_call(): pl.pallas_call(functools.partial(grad_kernel, starts), out_shape=out_shap...  14.1 us
    pallas_call x1, Pallas kernels, prob_call(): pl.pallas_call(prob_kernel, out_shape=(jax.ShapeDtypeStruct((SHARE, TOTAL...  13.3 us
    all_to_all x1, waiting for transfers between devices, local(): kterm = lax.all_to_all(kterm, CTX[:2] + HEAD, 0, 0, tiled=True)  12 us
    ppermute x16, starting transfers between devices, shift(): lax.ppermute(array, axis, [(i, (i + by) % size) for i in range(size)])  11 us
    ppermute x16, waiting for transfers between devices, shift(): lax.ppermute(array, axis, [(i, (i + by) % size) for i in range(size)])  10.8 us
    unnamed x28, local copies, waits for them, and re-layouts  9.53 us
    all_to_all x1, starting transfers between devices, local(): raw_0 = lax.all_to_all(raw_0, HEAD, 0, 0, tiled=True)  7.61 us
  transfers between devices with their start and end apart: 20, of which 9 were waited for; matrix products, arithmetic and copies ran while one was open for 1% of the time, Pallas kernels for 37%

profile of v2, /device:TPU:0, one launch (start us, length us, event | category | flops | bytes accessed | tf_op | source)
XLA Modules:
  0.0 146.6 jit_solution(12359261036914948479)
XLA Ops:
  0.7 1.2 copy.13
  1.9 0.9 pad_maximum_fusion.refs_0_
  2.9 3.2 %collective-permute-start.2 = (bf16[256,704]{1,0:T(8,128)(2,1)S(1)}, bf16[256,704]{1,0:T(8,128)(2,1)S(1)}, u32[]{:S(2)}, u32[]{:S(2)}) collective-permute-start(bf16[256,704]{1,0:T(8,128)(2,1)S(1)} %pad_maximum_fusion.refs_0_), channel_id=1, source_target_pairs={{0,48},{16,0},{32,16},{48,32},{1,49},{17,1},{33,17},{49,33},{2,50}... | collective-permute-start | bytes 1081352 | tf_op jit(solution)/shard_map/ppermute | solution.py:352
  6.1 1.9 %collective-permute-start = (bf16[256,704]{1,0:T(8,128)(2,1)S(1)}, bf16[256,704]{1,0:T(8,128)(2,1)S(1)}, u32[]{:S(2)}, u32[]{:S(2)}) collective-permute-start(bf16[256,704]{1,0:T(8,128)(2,1)S(1)} %pad_maximum_fusion.refs_0_), channel_id=1, source_target_pairs={{0,64},{64,0},{1,65},{65,1},{2,66},{66,2},{3,67},{67,3},{4,68},{68... | collective-permute-start | bytes 1081352 | tf_op jit(solution)/shard_map/ppermute | solution.py:352
  9.2 2.3 %copy-done.1 = bf16[256,16,576]{0,2,1:T(8,128)(2,1)S(1)} copy-done((bf16[256,16,576]{0,2,1:T(8,128)(2,1)S(1)}, bf16[256,16,576]{0,2,1:T(8,128)(2,1)}, u32[]{:S(2)}) %copy-start.1) | copy-done | bytes 4718616
  11.5 4.8 %mass_0.1 = (bf16[8,128,128]{2,1,0:T(8,128)(2,1)S(1)}, bf16[512,128]{1,0:T(8,128)(2,1)S(1)}) custom-call(s32[17]{0:T(128)S(1)} %stack.71.ids, s32[16]{0:T(128)S(1)} %copy-done.4, bf16[16,576,256]{2,1,0:T(8,128)(2,1)S(1)} %bitcast.23, f32[16,256]{1,0:T(8,128)S(1)} %bitcast.26, bf16[256,704]{1,0:T(8,128)(2,1)S(1)} %pad_maximum_fusion.refs_0_, ...), custom_call_target="tpu_custom_call" | custom-call | flops 3221225472 | bytes 5701632 | tf_op jit(solution)/shard_map/mass_0/pallas_call | solution.py:86
  16.4 2.1 %collective-permute-done.1.refs_1_ = bf16[256,704]{1,0:T(8,128)(2,1)S(1)} collective-permute-done((bf16[256,704]{1,0:T(8,128)(2,1)S(1)}, bf16[256,704]{1,0:T(8,128)(2,1)S(1)}, u32[]{:S(2)}, u32[]{:S(2)}) %collective-permute-start.1) | collective-permute-done | bytes 360480 | tf_op jit(solution)/shard_map/ppermute | solution.py:352
  19.0 3.2 %collective-permute-start.5 = (bf16[256,704]{1,0:T(8,128)(2,1)S(1)}, bf16[256,704]{1,0:T(8,128)(2,1)S(1)}, u32[]{:S(2)}, u32[]{:S(2)}) collective-permute-start(bf16[256,704]{1,0:T(8,128)(2,1)S(1)} %collective-permute-done.refs_0_), channel_id=1, source_target_pairs={{0,48},{16,0},{32,16},{48,32},{1,49},{17,1},{33,17},{49,33},{2,50}... | collective-permute-start | bytes 1081352 | tf_op jit(solution)/shard_map/ppermute | solution.py:352
  22.2 12.9 %mass_2.1 = (bf16[8,784,128]{2,1,0:T(8,128)(2,1)}, bf16[1536,128]{1,0:T(8,128)(2,1)S(1)}) custom-call(s32[17]{0:T(128)S(1)} %stack.71.ids, s32[16]{0:T(128)S(1)} %copy-done.4, bf16[16,576,256]{2,1,0:T(8,128)(2,1)S(1)} %bitcast.24, f32[16,256]{1,0:T(8,128)S(1)} %bitcast.27, bf16[256,704]{1,0:T(8,128)(2,1)S(1)} %collective-permute-done.refs_0_, ...), custom_call_target="tpu_custom_call" | custom-call | flops 9663676416 | bytes 7667712 | tf_op jit(solution)/shard_map/mass_2/pallas_call | solution.py:86
  35.1 0.8 copy-done.7
  35.9 4.2 %collective-permute-done.4.refs_0_ = bf16[256,704]{1,0:T(8,128)(2,1)S(1)} collective-permute-done((bf16[256,704]{1,0:T(8,128)(2,1)S(1)}, bf16[256,704]{1,0:T(8,128)(2,1)S(1)}, u32[]{:S(2)}, u32[]{:S(2)}) %collective-permute-start.4) | collective-permute-done | bytes 360480 | tf_op jit(solution)/shard_map/ppermute | solution.py:352
  40.7 0.7 collective-permute-start.13
  41.9 0.8 collective-permute-start.14
  42.7 7.6 %all-to-all-start = ((bf16[8,784,128]{2,1,0:T(8,128)(2,1)}), bf16[8,784,128]{2,1,0:T(8,128)(2,1)}, u32[]{:S(2)}, u32[]{:S(2)}) async-start(bf16[8,784,128]{2,1,0:T(8,128)(2,1)} %get-tuple-element.43), calls=%async_computation | async-start | bytes 3211264 | tf_op jit(solution)/shard_map/all_to_all | solution.py:398
  50.3 1.4 collective-permute-done.13.refs_6_
  51.7 2.6 %collective-permute-done.14.refs_7_ = bf16[256,704]{1,0:T(8,128)(2,1)S(1)} collective-permute-done((bf16[256,704]{1,0:T(8,128)(2,1)S(1)}, bf16[256,704]{1,0:T(8,128)(2,1)S(1)}, u32[]{:S(2)}, u32[]{:S(2)}) %collective-permute-start.14) | collective-permute-done | bytes 360480 | tf_op jit(solution)/shard_map/ppermute | solution.py:352
  54.2 2.3 %copy-done.2 = bf16[256,16,576]{0,2,1:T(8,128)(2,1)S(1)} copy-done((bf16[256,16,576]{0,2,1:T(8,128)(2,1)S(1)}, bf16[256,16,576]{0,2,1:T(8,128)(2,1)}, u32[]{:S(2)}) %copy-start.2) | copy-done | bytes 4718616
  56.6 16.1 %mass_8.1 = (bf16[8,512,128]{2,1,0:T(8,128)(2,1)}, bf16[2048,128]{1,0:T(8,128)(2,1)S(1)}) custom-call(s32[17]{0:T(128)S(1)} %stack.71.ids, s32[16]{0:T(128)S(1)} %copy-done.4, bf16[16,576,256]{2,1,0:T(8,128)(2,1)S(1)} %bitcast.25, f32[16,256]{1,0:T(8,128)S(1)} %bitcast.28, bf16[256,704]{1,0:T(8,128)(2,1)S(1)} %collective-permute-done.4.refs_0_, ...), custom_call_target="tpu_custom_call" | custom-call | flops 12884901888 | bytes 8650752 | tf_op jit(solution)/shard_map/mass_8/pallas_call | solution.py:86
  72.7 0.8 copy-done.6
  73.5 1.7 %all-to-all-done.qw_ref.refs_0_ = bf16[8,784,128]{2,1,0:T(8,128)(2,1)} async-done(((bf16[8,784,128]{2,1,0:T(8,128)(2,1)}), bf16[8,784,128]{2,1,0:T(8,128)(2,1)}, u32[]{:S(2)}, u32[]{:S(2)}) %all-to-all-start) | async-done | bytes 1605664 | tf_op jit(solution)/shard_map/all_to_all | solution.py:398
  75.2 5.9 %all-to-all-start.1 = ((bf16[8,512,128]{2,1,0:T(8,128)(2,1)}), bf16[8,512,128]{2,1,0:T(8,128)(2,1)S(1)}, u32[]{:S(2)}, u32[]{:S(2)}) async-start(bf16[8,512,128]{2,1,0:T(8,128)(2,1)} %get-tuple-element.53), calls=%async_computation.1 | async-start | bytes 2097152 | tf_op jit(solution)/shard_map/all_to_all | solution.py:400
  81.1 13.3 %probs.1 = (f32[32,4096]{1,0:T(8,128)}, bf16[4096,128]{1,0:T(8,128)(2,1)}, bf16[2048,4096]{1,0:T(8,128)(2,1)}) custom-call(s32[17]{0:T(128)} %copy-done, s32[16]{0:T(128)} %table.7, f32[32,128]{1,0:T(8,128)} %broadcast_in_dim.2.loss_ref, bf16[8,784,128]{2,1,0:T(8,128)(2,1)} %all-to-all-done.qw_ref.refs_0_, bf16[512,128]{1,0:T(8,128)(2,1)} %copy-done.5, ...), custom_call_target="tpu_custom_call" | custom-call | flops 8589934592 | bytes 20971520 | tf_op jit(solution)/shard_map/probs/pallas_call | solution.py:187
  94.4 2.1 %all-to-all-done.1.refs_1_ = bf16[8,512,128]{2,1,0:T(8,128)(2,1)S(1)} async-done(((bf16[8,512,128]{2,1,0:T(8,128)(2,1)}), bf16[8,512,128]{2,1,0:T(8,128)(2,1)S(1)}, u32[]{:S(2)}, u32[]{:S(2)}) %all-to-all-start.1) | async-done | bytes 1048608 | tf_op jit(solution)/shard_map/all_to_all | solution.py:400
  96.5 1.0 copy-done.9
  97.4 14.1 %grads.1 = (bf16[8,256,128]{2,1,0:T(8,128)(2,1)}, f32[2048,128]{1,0:T(8,128)}, f32[32,2048]{1,0:T(8,128)}, bf16[128,2048]{1,0:T(8,128)(2,1)}) custom-call(s32[17]{0:T(128)} %copy-done, f32[32,4096]{1,0:T(8,128)} %get-tuple-element.50.prob_ref, bf16[4096,128]{1,0:T(8,128)(2,1)} %get-tuple-element.51.keys_ref, bf16[2048,4096]{1,0:T(8,128)(2,1)} %get-tuple-element.52.gates_ref, ...), custom_call_target="tpu_custom_call" | custom-call | flops 6442450944 | bytes 27262976 | tf_op jit(solution)/shard_map/grads/pallas_call | solution.py:294
  111.5 5.1 %all-to-all-start.2 = ((bf16[8,256,128]{2,1,0:T(8,128)(2,1)}), bf16[8,256,128]{2,1,0:T(8,128)(2,1)S(1)}, u32[]{:S(2)}, u32[]{:S(2)}) async-start(bf16[8,256,128]{2,1,0:T(8,128)(2,1)} %get-tuple-element.54), calls=%async_computation.2 | async-start | bytes 1048576 | tf_op jit(solution)/shard_map/all_to_all | solution.py:407
  116.7 1.0 copy-done.8
  117.6 6.6 %kterms.1 = bf16[2048,128]{1,0:T(8,128)(2,1)} custom-call(s32[17]{0:T(128)} %copy-done, f32[32,2048]{1,0:T(8,128)} %get-tuple-element.55.half_ref, bf16[2048,4096]{1,0:T(8,128)(2,1)} %get-tuple-element.52.gates_ref, bf16[128,2048]{1,0:T(8,128)(2,1)} %get-tuple-element.56.q_t, f32[2048,128]{1,0:T(8,128)} %copy-done.8), custom_call_target="tpu_custom_call" | custom-call | flops 2147483648 | bytes 12582912 | tf_op jit(solution)/shard_map/kterms/pallas_call | solution.py:333
  124.3 3.7 %all-to-all-done.2 = bf16[8,256,128]{2,1,0:T(8,128)(2,1)S(1)} async-done(((bf16[8,256,128]{2,1,0:T(8,128)(2,1)}), bf16[8,256,128]{2,1,0:T(8,128)(2,1)S(1)}, u32[]{:S(2)}, u32[]{:S(2)}) %all-to-all-start.2) | async-done | bytes 524320 | tf_op jit(solution)/shard_map/all_to_all | solution.py:407
  127.9 4.9 %all-to-all-start.3 = ((bf16[64,32,128]{2,1,0:T(8,128)(2,1)}), bf16[64,32,128]{2,1,0:T(8,128)(2,1)S(1)}, u32[]{:S(2)}, u32[]{:S(2)}) async-start(bf16[64,32,128]{2,1,0:T(8,128)(2,1)} %bitcast.30), calls=%async_computation.3 | async-start | bytes 1048576 | tf_op jit(solution)/shard_map/all_to_all | solution.py:410
  132.8 1.0 convert.1
  133.9 12.0 %all-to-all-done.3 = bf16[64,32,128]{2,1,0:T(8,128)(2,1)S(1)} async-done(((bf16[64,32,128]{2,1,0:T(8,128)(2,1)}), bf16[64,32,128]{2,1,0:T(8,128)(2,1)S(1)}, u32[]{:S(2)}, u32[]{:S(2)}) %all-to-all-start.3) | async-done | bytes 524320 | tf_op jit(solution)/shard_map/all_to_all | solution.py:410
  (50 shorter events, 3.5 us)
Async XLA Ops:
  0.6 7.4 %copy-start.11 = (bf16[256,8]{0,1:T(8,128)(2,1)S(1)}, bf16[256,8]{0,1:T(8,128)(2,1)}, u32[]{:S(2)}) copy-start(bf16[256,8]{0,1:T(8,128)(2,1)} %param.13) | copy-start | bytes 12292
  0.6 7.6 %copy-start.10 = (bf16[256,8,128]{2,1,0:T(8,128)(2,1)S(1)}, bf16[256,8,128]{2,1,0:T(8,128)(2,1)}, u32[]{:S(2)}) copy-start(bf16[256,8,128]{2,1,0:T(8,128)(2,1)} %param.11) | copy-start | bytes 1572868
  1.9 6.4 %copy-start.12 = (f32[256]{0:T(256)S(1)}, f32[256]{0:T(256)}, u32[]{:S(2)}) copy-start(f32[256]{0:T(256)} %param.14) | copy-start | bytes 3076
  1.9 7.3 %copy-start.3 = (f32[256,16]{0,1:T(8,128)S(1)}, f32[256,16]{0,1:T(8,128)}, u32[]{:S(2)}) copy-start(f32[256,16]{0,1:T(8,128)} %param.10) | copy-start | bytes 49156
  1.9 7.3 %copy-start.4 = (s32[16]{0:T(128)S(1)}, s32[16]{0:T(128)}, u32[]{:S(2)}) copy-start(s32[16]{0:T(128)} %table.7) | copy-start | bytes 196
  2.8 6.4 %collective-permute-start.3 = (bf16[256,704]{1,0:T(8,128)(2,1)S(1)}, bf16[256,704]{1,0:T(8,128)(2,1)S(1)}, u32[]{:S(2)}, u32[]{:S(2)}) collective-permute-start(bf16[256,704]{1,0:T(8,128)(2,1)S(1)} %pad_maximum_fusion.refs_0_), channel_id=1, source_target_pairs={{0,8},{8,0},{1,9},{9,1},{2,10},{10,2},{3,11},{11,3},{4,12},{12,4},... | collective-permute-start | bytes 1081352 | tf_op jit(solution)/shard_map/ppermute | solution.py:352
  2.9 13.5 %collective-permute-start.2 = (bf16[256,704]{1,0:T(8,128)(2,1)S(1)}, bf16[256,704]{1,0:T(8,128)(2,1)S(1)}, u32[]{:S(2)}, u32[]{:S(2)}) collective-permute-start(bf16[256,704]{1,0:T(8,128)(2,1)S(1)} %pad_maximum_fusion.refs_0_), channel_id=1, source_target_pairs={{0,48},{16,0},{32,16},{48,32},{1,49},{17,1},{33,17},{49,33},{2,50}... | collective-permute-start | bytes 1081352 | tf_op jit(solution)/shard_map/ppermute | solution.py:352
  6.1 12.4 %collective-permute-start.1 = (bf16[256,704]{1,0:T(8,128)(2,1)S(1)}, bf16[256,704]{1,0:T(8,128)(2,1)S(1)}, u32[]{:S(2)}, u32[]{:S(2)}) collective-permute-start(bf16[256,704]{1,0:T(8,128)(2,1)S(1)} %pad_maximum_fusion.refs_0_), channel_id=1, source_target_pairs={{0,16},{16,32},{32,48},{48,0},{1,17},{17,33},{33,49},{49,1},{2,18}... | collective-permute-start | bytes 1081352 | tf_op jit(solution)/shard_map/ppermute | solution.py:352
  6.1 12.4 %collective-permute-start = (bf16[256,704]{1,0:T(8,128)(2,1)S(1)}, bf16[256,704]{1,0:T(8,128)(2,1)S(1)}, u32[]{:S(2)}, u32[]{:S(2)}) collective-permute-start(bf16[256,704]{1,0:T(8,128)(2,1)S(1)} %pad_maximum_fusion.refs_0_), channel_id=1, source_target_pairs={{0,64},{64,0},{1,65},{65,1},{2,66},{66,2},{3,67},{67,3},{4,68},{68... | collective-permute-start | bytes 1081352 | tf_op jit(solution)/shard_map/ppermute | solution.py:352
  8.5 45.7 %copy-start = (s32[17]{0:T(128)}, s32[17]{0:T(128)S(1)}, u32[]{:S(2)}) copy-start(s32[17]{0:T(128)S(1)} %stack.71.ids) | copy-start | bytes 208
  9.2 2.3 %copy-start.1 = (bf16[256,16,576]{0,2,1:T(8,128)(2,1)S(1)}, bf16[256,16,576]{0,2,1:T(8,128)(2,1)}, u32[]{:S(2)}) copy-start(bf16[256,16,576]{0,2,1:T(8,128)(2,1)} %param.8) | copy-start | bytes 14155780
  16.3 18.8 %copy-start.5 = (bf16[512,128]{1,0:T(8,128)(2,1)}, bf16[512,128]{1,0:T(8,128)(2,1)S(1)}, u32[]{:S(2)}) copy-start(bf16[512,128]{1,0:T(8,128)(2,1)S(1)} %get-tuple-element.44.refs_0_) | copy-start | bytes 393220
  18.5 3.8 %collective-permute-start.9 = (bf16[256,704]{1,0:T(8,128)(2,1)S(1)}, bf16[256,704]{1,0:T(8,128)(2,1)S(1)}, u32[]{:S(2)}, u32[]{:S(2)}) collective-permute-start(bf16[256,704]{1,0:T(8,128)(2,1)S(1)} %collective-permute-done.2.refs_2_), channel_id=1, source_target_pairs={{0,8},{8,0},{1,9},{9,1},{2,10},{10,2},{3,11},{11,3},{4,12},{12,4},... | collective-permute-start | bytes 1081352 | tf_op jit(solution)/shard_map/ppermute | solution.py:352
  18.5 3.8 %collective-permute-start.8 = (bf16[256,704]{1,0:T(8,128)(2,1)S(1)}, bf16[256,704]{1,0:T(8,128)(2,1)S(1)}, u32[]{:S(2)}, u32[]{:S(2)}) collective-permute-start(bf16[256,704]{1,0:T(8,128)(2,1)S(1)} %collective-permute-done.1.refs_1_), channel_id=1, source_target_pairs={{0,8},{8,0},{1,9},{9,1},{2,10},{10,2},{3,11},{11,3},{4,12},{12,4},... | collective-permute-start | bytes 1081352 | tf_op jit(solution)/shard_map/ppermute | solution.py:352
  19.0 3.3 %collective-permute-start.7 = (bf16[256,704]{1,0:T(8,128)(2,1)S(1)}, bf16[256,704]{1,0:T(8,128)(2,1)S(1)}, u32[]{:S(2)}, u32[]{:S(2)}) collective-permute-start(bf16[256,704]{1,0:T(8,128)(2,1)S(1)} %collective-permute-done.refs_0_), channel_id=1, source_target_pairs={{0,8},{8,0},{1,9},{9,1},{2,10},{10,2},{3,11},{11,3},{4,12},{12,4},... | collective-permute-start | bytes 1081352 | tf_op jit(solution)/shard_map/ppermute | solution.py:352
  19.0 16.9 %collective-permute-start.6 = (bf16[256,704]{1,0:T(8,128)(2,1)S(1)}, bf16[256,704]{1,0:T(8,128)(2,1)S(1)}, u32[]{:S(2)}, u32[]{:S(2)}) collective-permute-start(bf16[256,704]{1,0:T(8,128)(2,1)S(1)} %collective-permute-done.1.refs_1_), channel_id=1, source_target_pairs={{0,16},{16,32},{32,48},{48,0},{1,17},{17,33},{33,49},{49,1},{2,18}... | collective-permute-start | bytes 1081352 | tf_op jit(solution)/shard_map/ppermute | solution.py:352
  19.0 16.9 %collective-permute-start.5 = (bf16[256,704]{1,0:T(8,128)(2,1)S(1)}, bf16[256,704]{1,0:T(8,128)(2,1)S(1)}, u32[]{:S(2)}, u32[]{:S(2)}) collective-permute-start(bf16[256,704]{1,0:T(8,128)(2,1)S(1)} %collective-permute-done.refs_0_), channel_id=1, source_target_pairs={{0,48},{16,0},{32,16},{48,32},{1,49},{17,1},{33,17},{49,33},{2,50}... | collective-permute-start | bytes 1081352 | tf_op jit(solution)/shard_map/ppermute | solution.py:352
  22.2 17.9 %collective-permute-start.4 = (bf16[256,704]{1,0:T(8,128)(2,1)S(1)}, bf16[256,704]{1,0:T(8,128)(2,1)S(1)}, u32[]{:S(2)}, u32[]{:S(2)}) collective-permute-start(bf16[256,704]{1,0:T(8,128)(2,1)S(1)} %collective-permute-done.refs_0_), channel_id=1, source_target_pairs={{0,16},{16,32},{32,48},{48,0},{1,17},{17,33},{33,49},{49,1},{2,18}... | collective-permute-start | bytes 1081352 | tf_op jit(solution)/shard_map/ppermute | solution.py:352
  40.1 1.7 %collective-permute-start.10 = (bf16[256,704]{1,0:T(8,128)(2,1)S(1)}, bf16[256,704]{1,0:T(8,128)(2,1)S(1)}, u32[]{:S(2)}, u32[]{:S(2)}) collective-permute-start(bf16[256,704]{1,0:T(8,128)(2,1)S(1)} %collective-permute-done.4.refs_0_), channel_id=1, source_target_pairs={{0,8},{8,0},{1,9},{9,1},{2,10},{10,2},{3,11},{11,3},{4,12},{12,4},... | collective-permute-start | bytes 1081352 | tf_op jit(solution)/shard_map/ppermute | solution.py:352
  40.1 10.2 %collective-permute-start.12 = (bf16[256,704]{1,0:T(8,128)(2,1)S(1)}, bf16[256,704]{1,0:T(8,128)(2,1)S(1)}, u32[]{:S(2)}, u32[]{:S(2)}) collective-permute-start(bf16[256,704]{1,0:T(8,128)(2,1)S(1)} %collective-permute-done.6.refs_2_), channel_id=1, source_target_pairs={{0,8},{8,0},{1,9},{9,1},{2,10},{10,2},{3,11},{11,3},{4,12},{12,4},... | collective-permute-start | bytes 1081352 | tf_op jit(solution)/shard_map/ppermute | solution.py:352
  40.7 11.0 %collective-permute-start.13 = (bf16[256,704]{1,0:T(8,128)(2,1)S(1)}, bf16[256,704]{1,0:T(8,128)(2,1)S(1)}, u32[]{:S(2)}, u32[]{:S(2)}) collective-permute-start(bf16[256,704]{1,0:T(8,128)(2,1)S(1)} %collective-permute-done.5.refs_1_), channel_id=1, source_target_pairs={{0,48},{16,0},{32,16},{48,32},{1,49},{17,1},{33,17},{49,33},{2,50}... | collective-permute-start | bytes 1081352 | tf_op jit(solution)/shard_map/ppermute | solution.py:352
  41.4 10.3 %collective-permute-start.11 = (bf16[256,704]{1,0:T(8,128)(2,1)S(1)}, bf16[256,704]{1,0:T(8,128)(2,1)S(1)}, u32[]{:S(2)}, u32[]{:S(2)}) collective-permute-start(bf16[256,704]{1,0:T(8,128)(2,1)S(1)} %collective-permute-done.5.refs_1_), channel_id=1, source_target_pairs={{0,8},{8,0},{1,9},{9,1},{2,10},{10,2},{3,11},{11,3},{4,12},{12,4},... | collective-permute-start | bytes 1081352 | tf_op jit(solution)/shard_map/ppermute | solution.py:352
  41.9 12.4 %collective-permute-start.14 = (bf16[256,704]{1,0:T(8,128)(2,1)S(1)}, bf16[256,704]{1,0:T(8,128)(2,1)S(1)}, u32[]{:S(2)}, u32[]{:S(2)}) collective-permute-start(bf16[256,704]{1,0:T(8,128)(2,1)S(1)} %collective-permute-done.10.refs_3_), channel_id=1, source_target_pairs={{0,16},{16,32},{32,48},{48,0},{1,17},{17,33},{33,49},{49,1},{2,18}... | collective-permute-start | bytes 1081352 | tf_op jit(solution)/shard_map/ppermute | solution.py:352
  42.7 32.5 %all-to-all-start = ((bf16[8,784,128]{2,1,0:T(8,128)(2,1)}), bf16[8,784,128]{2,1,0:T(8,128)(2,1)}, u32[]{:S(2)}, u32[]{:S(2)}) async-start(bf16[8,784,128]{2,1,0:T(8,128)(2,1)} %get-tuple-element.43), calls=%async_computation | async-start | bytes 3211264 | tf_op jit(solution)/shard_map/all_to_all | solution.py:398
  54.2 2.3 %copy-start.2 = (bf16[256,16,576]{0,2,1:T(8,128)(2,1)S(1)}, bf16[256,16,576]{0,2,1:T(8,128)(2,1)}, u32[]{:S(2)}) copy-start(bf16[256,16,576]{0,2,1:T(8,128)(2,1)} %param.8) | copy-start | bytes 14155780
  72.7 0.8 copy-start.6
  75.2 21.3 %all-to-all-start.1 = ((bf16[8,512,128]{2,1,0:T(8,128)(2,1)}), bf16[8,512,128]{2,1,0:T(8,128)(2,1)S(1)}, u32[]{:S(2)}, u32[]{:S(2)}) async-start(bf16[8,512,128]{2,1,0:T(8,128)(2,1)} %get-tuple-element.53), calls=%async_computation.1 | async-start | bytes 2097152 | tf_op jit(solution)/shard_map/all_to_all | solution.py:400
  96.5 1.0 copy-start.9
  111.5 5.1 %collective-permute-start.15 = (f32[2048,128]{1,0:T(8,128)}, f32[2048,128]{1,0:T(8,128)S(1)}, u32[]{:S(2)}, u32[]{:S(2)}) collective-permute-start(f32[2048,128]{1,0:T(8,128)} %get-tuple-element.57), channel_id=1, source_target_pairs={{0,8},{8,0},{1,9},{9,1},{2,10},{10,2},{3,11},{11,3},{4,12},{12,4},... | collective-permute-start | bytes 3145736 | tf_op jit(solution)/shard_map/ppermute | solution.py:352
  111.5 16.4 %all-to-all-start.2 = ((bf16[8,256,128]{2,1,0:T(8,128)(2,1)}), bf16[8,256,128]{2,1,0:T(8,128)(2,1)S(1)}, u32[]{:S(2)}, u32[]{:S(2)}) async-start(bf16[8,256,128]{2,1,0:T(8,128)(2,1)} %get-tuple-element.54), calls=%async_computation.2 | async-start | bytes 1048576 | tf_op jit(solution)/shard_map/all_to_all | solution.py:407
  116.7 1.0 copy-start.8
  127.9 18.0 %all-to-all-start.3 = ((bf16[64,32,128]{2,1,0:T(8,128)(2,1)}), bf16[64,32,128]{2,1,0:T(8,128)(2,1)S(1)}, u32[]{:S(2)}, u32[]{:S(2)}) async-start(bf16[64,32,128]{2,1,0:T(8,128)(2,1)} %bitcast.30), calls=%async_computation.3 | async-start | bytes 1048576 | tf_op jit(solution)/shard_map/all_to_all | solution.py:410
  (1 other events, 0.8 us)

commit v3 on v2

--- a/solution.py
+++ b/solution.py
@@ -39,6 +39,10 @@
 VMEM = pltpu.VMEM
 
 
+def in_hbm(array):
+    return pltpu.with_memory_space_constraint(array, pltpu.HBM)
+
+
 def mass_kernel(first, count, carried, hstep, ids, table, q_ref, lse_ref, *refs):
     blocks, extra = refs[:count], refs[count : count + carried]
     out_ref, keys_ref, acc = refs[count + carried :]
@@ -87,7 +91,7 @@
         functools.partial(mass_kernel, first, count, len(extra), hstep),
         out_shape=(
             jax.ShapeDtypeStruct((PEERS, rows, IDIM), jnp.bfloat16),
-            jax.ShapeDtypeStruct((count * ROWS, IDIM), jnp.bfloat16),
+            pltpu.HBM((count * ROWS, IDIM), jnp.bfloat16),
         ),
         grid_spec=pltpu.PrefetchScalarGridSpec(
             num_scalar_prefetch=2,
@@ -148,7 +152,7 @@
         for i in range(count):
             cols = slice(i * IDIM, (i + 1) * IDIM)
             gate = jnp.where(dots[:, cols] > 0, w, jnp.float32(0.0))
-            gates_ref[rows, cols] = gate.astype(jnp.bfloat16)
+            gates_ref[0, rows, cols] = gate.astype(jnp.bfloat16)
             y = gate * dots[:, cols]
             acc[i] = y if acc[i] is None else acc[i] + y
     for i in range(count):
@@ -189,7 +193,7 @@
         out_shape=(
             jax.ShapeDtypeStruct((SHARE, TOTAL), jnp.float32),
             jax.ShapeDtypeStruct((TOTAL, IDIM), jnp.bfloat16),
-            jax.ShapeDtypeStruct((PEERS * ROWS, TOTAL), jnp.bfloat16),
+            jax.ShapeDtypeStruct((TOTAL // WIDE, PEERS * ROWS, WIDE), jnp.bfloat16),
         ),
         grid_spec=pltpu.PrefetchScalarGridSpec(
             num_scalar_prefetch=2,
@@ -202,7 +206,7 @@
             out_specs=(
                 pl.BlockSpec((SHARE, TOTAL), lambda i, *_: (0, 0)),
                 pl.BlockSpec((TOTAL, IDIM), lambda i, *_: (0, 0)),
-                pl.BlockSpec((PEERS * ROWS, WIDE), lambda i, *_: (0, i)),
+                pl.BlockSpec((1, PEERS * ROWS, WIDE), lambda i, *_: (i, 0, 0)),
             ),
             scratch_shapes=[
                 pltpu.VMEM((PEERS, ROWS, IDIM), jnp.float32),
@@ -221,7 +225,7 @@
     g = jnp.broadcast_to(g[:, None, :], (SHARE, PEERS, WIDE)).reshape(ROWS, WIDE)
     for h in range(PEERS):
         part = slice(h * ROWS, (h + 1) * ROWS)
-        coefs[part, :] = (g * gates_ref[part, :].astype(jnp.float32)).astype(jnp.bfloat16)
+        coefs[part, :] = (g * gates_ref[0, part, :].astype(jnp.float32)).astype(jnp.bfloat16)
 
 
 def kterm_tile(coefs, q_t):
@@ -281,15 +285,15 @@
     return pl.BlockSpec(a.shape, lambda i, *_: (0,) * len(a.shape))
 
 
-GATES = pl.BlockSpec((PEERS * ROWS, WIDE), lambda i, *_: (0, i))
+GATES = pl.BlockSpec((1, PEERS * ROWS, WIDE), lambda i, *_: (i, 0, 0))
 
 
 def grad_call(ids, prob, keys, gates, loss, raws, starts):
     out_shape = (
         jax.ShapeDtypeStruct((PEERS, ROWS, IDIM), jnp.bfloat16),
         jax.ShapeDtypeStruct((HALF, IDIM), jnp.float32),
-        jax.ShapeDtypeStruct((SHARE, HALF), jnp.float32),
-        jax.ShapeDtypeStruct((IDIM, PEERS * ROWS), jnp.bfloat16),
+        pltpu.HBM((SHARE, HALF), jnp.float32),
+        pltpu.HBM((IDIM, PEERS * ROWS), jnp.bfloat16),
     )
     return pl.pallas_call(
         functools.partial(grad_kernel, starts),
@@ -305,12 +309,12 @@
                 pltpu.VMEM((PEERS * ROWS, WIDE), jnp.bfloat16),
             ],
         ),
-        compiler_params=pltpu.CompilerParams(vmem_limit_bytes=60 * MIB),
+        compiler_params=pltpu.CompilerParams(vmem_limit_bytes=50 * MIB),
         cost_estimate=pl.CostEstimate(
             flops=6 * PEERS * ROWS * TOTAL * IDIM, bytes_accessed=26 * MIB, transcendentals=0
         ),
         name="grads",
-    )(ids, prob, keys, gates, loss, *raws)
+    )(ids, in_hbm(prob), in_hbm(keys), in_hbm(gates), loss, *raws)
 
 
 def kterm_kernel(ids, half_ref, gates_ref, q_t, other_ref, out_ref, coefs):
@@ -340,12 +344,12 @@
             out_specs=whole(out),
             scratch_shapes=[pltpu.VMEM((PEERS * ROWS, WIDE), jnp.bfloat16)],
         ),
-        compiler_params=pltpu.CompilerParams(vmem_limit_bytes=60 * MIB),
+        compiler_params=pltpu.CompilerParams(vmem_limit_bytes=50 * MIB),
         cost_estimate=pl.CostEstimate(
             flops=2 * PEERS * ROWS * TOTAL * IDIM, bytes_accessed=12 * MIB, transcendentals=0
         ),
         name="kterms",
-    )(ids, half, gates, q_t, other)
+    )(ids, in_hbm(half), in_hbm(gates), in_hbm(q_t), other)
 
 
 def shift(array, axis, size, by):
@@ -392,14 +396,15 @@
     zyp, zym, y2 = up(z), down(z), up(yp)
     pz, pyp, pym = core(z), core(yp), core(ym)
     raw_0, keys_1 = mass([z, yp, ym, pz, pyp, pym], 2, (qw, near))
-    zyp, zym, y2, raw_0 = lax.optimization_barrier((zyp, zym, y2, raw_0))
+    zyp, zym, raw_0 = lax.optimization_barrier((zyp, zym, raw_0))
     pzyp, pzym, py2 = core(zyp), core(zym), core(y2)
     zy2, pzy2 = down(zym), up(pzyp)
     raw_0 = lax.all_to_all(raw_0, HEAD, 0, 0, tiled=True)
-    raw_1, keys_2 = mass([zyp, zym, y2, pzyp, pzym, py2, zy2, pzy2], 8)
+    far, keys_2 = mass([zyp, zym, y2, pzyp, pzym, py2], 8)
+    raw_1, keys_3 = mass([zy2, pzy2], 14, (far,))
     raw_1 = lax.all_to_all(raw_1, HEAD, 0, 0, tiled=True)
 
-    prob, keys, gates = prob_call(ids, block_offsets, loss, raw_0, (keys_0, keys_1, keys_2))
+    prob, keys, gates = prob_call(ids, block_offsets, loss, raw_0, (keys_0, keys_1, keys_2, keys_3))
     qgrad, other, half, i_t = grad_call(
         ids, prob, keys, gates, loss, (raw_0, raw_1), (ROWS + PAD, 0)
     )

time: 147 us -> 143 us (0.973)
  local copies, waits for them, and re-layouts: 10.5 us -> 7.02 us
  waiting for transfers between devices: 30.3 us -> 28.2 us
  Pallas kernels: 67.8 us -> 69.4 us
    ppermute x16, waiting for transfers between devices: 10.8 us -> 6.43 us  [shift(): lax.ppermute(array, axis, [(i, (i + by) % size) for i in range(size)])]
    unnamed x28 -> x22, local copies, waits for them, and re-layouts: 9.53 us -> 6.05 us
    pallas_call x3 -> x4, Pallas kernels: 33.8 us -> 36.6 us  [mass_call(): pl.pallas_call(functools.partial(mass_kernel, first, count, len(extra), h...]
    all_to_all x1, starting transfers between devices: 5.89 us -> 4.31 us  [local(): raw_1 = lax.all_to_all(raw_1, HEAD, 0, 0, tiled=True)]
  transfers between devices with their start and end apart: 20 -> 20, of which waited for: 9 -> 6; matrix products, arithmetic and copies ran while one was open for 1% -> 2% of each run, Pallas kernels for 37% -> 39%
where the time goes in v3:
time: 143 us
  Pallas kernels  69.4 us (49%)
  starting transfers between devices  34.7 us (24%)
  waiting for transfers between devices  28.2 us (20%)
  local copies, waits for them, and re-layouts  7.02 us (5%)
  other arithmetic  2.68 us (2%)
    pallas_call x4, Pallas kernels, mass_call(): pl.pallas_call(functools.partial(mass_kernel, first, count, len(extra), h...  36.6 us
    pallas_call x1, Pallas kernels, grad_call(): pl.pallas_call(functools.partial(grad_kernel, starts), out_shape=out_shap...  13.3 us
    pallas_call x1, Pallas kernels, prob_call(): pl.pallas_call(prob_kernel, out_shape=(jax.ShapeDtypeStruct((SHARE, TOTAL...  13.2 us
    all_to_all x1, waiting for transfers between devices, local(): kterm = lax.all_to_all(kterm, CTX[:2] + HEAD, 0, 0, tiled=True)  11.7 us
    ppermute x16, starting transfers between devices, shift(): lax.ppermute(array, axis, [(i, (i + by) % size) for i in range(size)])  11.5 us
    all_to_all x1, starting transfers between devices, local(): raw_0 = lax.all_to_all(raw_0, HEAD, 0, 0, tiled=True)  7.61 us
    ppermute x16, waiting for transfers between devices, shift(): lax.ppermute(array, axis, [(i, (i + by) % size) for i in range(size)])  6.43 us
    pallas_call x1, Pallas kernels, kterm_call(): pl.pallas_call(kterm_kernel, out_shape=out, grid_spec=pltpu.PrefetchScala...  6.2 us
  transfers between devices with their start and end apart: 20, of which 6 were waited for; matrix products, arithmetic and copies ran while one was open for 2% of the time, Pallas kernels for 39%

profile of v3, /device:TPU:0, one launch (start us, length us, event | category | flops | bytes accessed | tf_op | source)
XLA Modules:
  0.0 142.8 jit_solution(1161872723510969184)
XLA Ops:
  0.7 1.2 copy.13
  1.9 0.9 pad_maximum_fusion.refs_0_
  2.9 3.2 %collective-permute-start.2 = (bf16[256,704]{1,0:T(8,128)(2,1)S(1)}, bf16[256,704]{1,0:T(8,128)(2,1)S(1)}, u32[]{:S(2)}, u32[]{:S(2)}) collective-permute-start(bf16[256,704]{1,0:T(8,128)(2,1)S(1)} %pad_maximum_fusion.refs_0_), channel_id=1, source_target_pairs={{0,48},{16,0},{32,16},{48,32},{1,49},{17,1},{33,17},{49,33},{2,50}... | collective-permute-start | bytes 1081352 | tf_op jit(solution)/shard_map/ppermute | solution.py:356
  6.1 1.9 %collective-permute-start = (bf16[256,704]{1,0:T(8,128)(2,1)S(1)}, bf16[256,704]{1,0:T(8,128)(2,1)S(1)}, u32[]{:S(2)}, u32[]{:S(2)}) collective-permute-start(bf16[256,704]{1,0:T(8,128)(2,1)S(1)} %pad_maximum_fusion.refs_0_), channel_id=1, source_target_pairs={{0,64},{64,0},{1,65},{65,1},{2,66},{66,2},{3,67},{67,3},{4,68},{68... | collective-permute-start | bytes 1081352 | tf_op jit(solution)/shard_map/ppermute | solution.py:356
  8.1 0.1 reshape.18
  8.5 0.7 broadcast_in_dim.2.loss_ref
  9.2 2.3 %copy-done.3 = bf16[256,16,576]{0,2,1:T(8,128)(2,1)S(1)} copy-done((bf16[256,16,576]{0,2,1:T(8,128)(2,1)S(1)}, bf16[256,16,576]{0,2,1:T(8,128)(2,1)}, u32[]{:S(2)}) %copy-start.3) | copy-done | bytes 4718616
  11.5 5.5 %mass_0.1 = (bf16[8,128,128]{2,1,0:T(8,128)(2,1)S(1)}, bf16[512,128]{1,0:T(8,128)(2,1)}) custom-call(s32[17]{0:T(128)S(1)} %stack.71.ids, s32[16]{0:T(128)S(1)} %copy-done.6, bf16[16,576,256]{2,1,0:T(8,128)(2,1)S(1)} %bitcast.23, f32[16,256]{1,0:T(8,128)S(1)} %bitcast.27, bf16[256,704]{1,0:T(8,128)(2,1)S(1)} %pad_maximum_fusion.refs_0_, ...), custom_call_target="tpu_custom_call" | custom-call | flops 3221225472 | bytes 5701632 | tf_op jit(solution)/shard_map/mass_0/pallas_call | solution.py:90
  17.0 1.5 %collective-permute-done.1.refs_1_ = bf16[256,704]{1,0:T(8,128)(2,1)S(1)} collective-permute-done((bf16[256,704]{1,0:T(8,128)(2,1)S(1)}, bf16[256,704]{1,0:T(8,128)(2,1)S(1)}, u32[]{:S(2)}, u32[]{:S(2)}) %collective-permute-start.1) | collective-permute-done | bytes 360480 | tf_op jit(solution)/shard_map/ppermute | solution.py:356
  18.5 0.5 collective-permute-start.7
  19.0 3.2 %collective-permute-start.5 = (bf16[256,704]{1,0:T(8,128)(2,1)S(1)}, bf16[256,704]{1,0:T(8,128)(2,1)S(1)}, u32[]{:S(2)}, u32[]{:S(2)}) collective-permute-start(bf16[256,704]{1,0:T(8,128)(2,1)S(1)} %collective-permute-done.refs_0_), channel_id=1, source_target_pairs={{0,48},{16,0},{32,16},{48,32},{1,49},{17,1},{33,17},{49,33},{2,50}... | collective-permute-start | bytes 1081352 | tf_op jit(solution)/shard_map/ppermute | solution.py:356
  22.2 13.0 %mass_2.1 = (bf16[8,784,128]{2,1,0:T(8,128)(2,1)}, bf16[1536,128]{1,0:T(8,128)(2,1)}) custom-call(s32[17]{0:T(128)S(1)} %stack.71.ids, s32[16]{0:T(128)S(1)} %copy-done.6, bf16[16,576,256]{2,1,0:T(8,128)(2,1)S(1)} %bitcast.24, f32[16,256]{1,0:T(8,128)S(1)} %bitcast.28, bf16[256,704]{1,0:T(8,128)(2,1)S(1)} %collective-permute-done.refs_0_, ...), custom_call_target="tpu_custom_call" | custom-call | flops 9663676416 | bytes 7667712 | tf_op jit(solution)/shard_map/mass_2/pallas_call | solution.py:90
  35.2 4.9 %collective-permute-done.4.refs_0_ = bf16[256,704]{1,0:T(8,128)(2,1)S(1)} collective-permute-done((bf16[256,704]{1,0:T(8,128)(2,1)S(1)}, bf16[256,704]{1,0:T(8,128)(2,1)S(1)}, u32[]{:S(2)}, u32[]{:S(2)}) %collective-permute-start.4) | collective-permute-done | bytes 360480 | tf_op jit(solution)/shard_map/ppermute | solution.py:356
  40.1 0.5 collective-permute-start.12
  40.7 7.6 %all-to-all-start = ((bf16[8,784,128]{2,1,0:T(8,128)(2,1)}), bf16[8,784,128]{2,1,0:T(8,128)(2,1)}, u32[]{:S(2)}, u32[]{:S(2)}) async-start(bf16[8,784,128]{2,1,0:T(8,128)(2,1)} %get-tuple-element.44), calls=%async_computation | async-start | bytes 3211264 | tf_op jit(solution)/shard_map/all_to_all | solution.py:402
  48.3 0.5 collective-permute-start.13
  48.8 1.5 %collective-permute-start.14 = (bf16[256,704]{1,0:T(8,128)(2,1)S(1)}, bf16[256,704]{1,0:T(8,128)(2,1)S(1)}, u32[]{:S(2)}, u32[]{:S(2)}) collective-permute-start(bf16[256,704]{1,0:T(8,128)(2,1)S(1)} %collective-permute-done.10.refs_3_), channel_id=1, source_target_pairs={{0,16},{16,32},{32,48},{48,0},{1,17},{17,33},{33,49},{49,1},{2,18}... | collective-permute-start | bytes 1081352 | tf_op jit(solution)/shard_map/ppermute | solution.py:356
  50.3 2.3 %copy-done.4 = bf16[256,16,576]{0,2,1:T(8,128)(2,1)S(1)} copy-done((bf16[256,16,576]{0,2,1:T(8,128)(2,1)S(1)}, bf16[256,16,576]{0,2,1:T(8,128)(2,1)}, u32[]{:S(2)}) %copy-start.4) | copy-done | bytes 4718616
  52.7 12.4 %mass_8.1 = (bf16[8,384,128]{2,1,0:T(8,128)(2,1)S(1)}, bf16[1536,128]{1,0:T(8,128)(2,1)}) custom-call(s32[17]{0:T(128)S(1)} %stack.71.ids, s32[16]{0:T(128)S(1)} %copy-done.6, bf16[16,576,256]{2,1,0:T(8,128)(2,1)S(1)} %bitcast.25, f32[16,256]{1,0:T(8,128)S(1)} %bitcast.29, bf16[256,704]{1,0:T(8,128)(2,1)S(1)} %collective-permute-done.4.refs_0_, ...), custom_call_target="tpu_custom_call" | custom-call | flops 9663676416 | bytes 7667712 | tf_op jit(solution)/shard_map/mass_8/pallas_call | solution.py:90
  65.1 5.8 %mass_14.1 = (bf16[8,512,128]{2,1,0:T(8,128)(2,1)}, bf16[512,128]{1,0:T(8,128)(2,1)}) custom-call(s32[17]{0:T(128)S(1)} %stack.71.ids, s32[16]{0:T(128)S(1)} %copy-done.6, bf16[16,576,256]{2,1,0:T(8,128)(2,1)S(1)} %bitcast.26, f32[16,256]{1,0:T(8,128)S(1)} %bitcast.30, bf16[256,704]{1,0:T(8,128)(2,1)S(1)} %collective-permute-done.13.refs_0_, ...), custom_call_target="tpu_custom_call" | custom-call | flops 3221225472 | bytes 5701632 | tf_op jit(solution)/shard_map/mass_14/pallas_call | solution.py:90
  70.9 2.9 %all-to-all-done.qw_ref.refs_0_ = bf16[8,784,128]{2,1,0:T(8,128)(2,1)} async-done(((bf16[8,784,128]{2,1,0:T(8,128)(2,1)}), bf16[8,784,128]{2,1,0:T(8,128)(2,1)}, u32[]{:S(2)}, u32[]{:S(2)}) %all-to-all-start) | async-done | bytes 1605664 | tf_op jit(solution)/shard_map/all_to_all | solution.py:402
  73.8 4.3 %all-to-all-start.1 = ((bf16[8,512,128]{2,1,0:T(8,128)(2,1)}), bf16[8,512,128]{2,1,0:T(8,128)(2,1)S(1)}, u32[]{:S(2)}, u32[]{:S(2)}) async-start(bf16[8,512,128]{2,1,0:T(8,128)(2,1)} %get-tuple-element.55), calls=%async_computation.1 | async-start | bytes 2097152 | tf_op jit(solution)/shard_map/all_to_all | solution.py:405
  78.1 13.2 %probs.1 = (f32[32,4096]{1,0:T(8,128)}, bf16[4096,128]{1,0:T(8,128)(2,1)}, bf16[4,2048,1024]{2,1,0:T(8,128)(2,1)}) custom-call(s32[17]{0:T(128)} %copy-done.1, s32[16]{0:T(128)} %table.9, f32[32,128]{1,0:T(8,128)} %broadcast_in_dim.2.loss_ref, bf16[8,784,128]{2,1,0:T(8,128)(2,1)} %all-to-all-done.qw_ref.refs_0_, bf16[512,128]{1,0:T(8,128)(2,1)} %get-tuple-element.45.refs_0_, ...), custom_call_target="tpu_custom_call" | custom-call | flops 8589934592 | bytes 20971520 | tf_op jit(solution)/shard_map/probs/pallas_call | solution.py:191
  91.3 2.1 %all-to-all-done.1.refs_1_ = bf16[8,512,128]{2,1,0:T(8,128)(2,1)S(1)} async-done(((bf16[8,512,128]{2,1,0:T(8,128)(2,1)}), bf16[8,512,128]{2,1,0:T(8,128)(2,1)S(1)}, u32[]{:S(2)}, u32[]{:S(2)}) %all-to-all-start.1) | async-done | bytes 1048608 | tf_op jit(solution)/shard_map/all_to_all | solution.py:405
  93.4 13.3 %grads.1 = (bf16[8,256,128]{2,1,0:T(8,128)(2,1)}, f32[2048,128]{1,0:T(8,128)S(1)}, f32[32,2048]{1,0:T(8,128)}, bf16[128,2048]{1,0:T(8,128)(2,1)}) custom-call(s32[17]{0:T(128)S(1)} %copy-done.2, f32[32,4096]{1,0:T(8,128)} %get-tuple-element.52.prob_ref, bf16[4096,128]{1,0:T(8,128)(2,1)} %get-tuple-element.53.keys_ref, ...), custom_call_target="tpu_custom_call" | custom-call | flops 6442450944 | bytes 27262976 | tf_op jit(solution)/shard_map/grads/pallas_call | solution.py:298
  106.8 5.2 %all-to-all-start.2 = ((bf16[8,256,128]{2,1,0:T(8,128)(2,1)}), bf16[8,256,128]{2,1,0:T(8,128)(2,1)S(1)}, u32[]{:S(2)}, u32[]{:S(2)}) async-start(bf16[8,256,128]{2,1,0:T(8,128)(2,1)} %get-tuple-element.56), calls=%async_computation.2 | async-start | bytes 1048576 | tf_op jit(solution)/shard_map/all_to_all | solution.py:412
  112.0 6.2 %kterms.1 = bf16[2048,128]{1,0:T(8,128)(2,1)} custom-call(s32[17]{0:T(128)S(1)} %copy-done.2, f32[32,2048]{1,0:T(8,128)} %get-tuple-element.57.half_ref, bf16[4,2048,1024]{2,1,0:T(8,128)(2,1)} %get-tuple-element.54.gates_ref, bf16[128,2048]{1,0:T(8,128)(2,1)} %get-tuple-element.58.q_t, f32[2048,128]{1,0:T(8,128)S(1)} %collective-permute-done.15.other_ref), custom_call_target="tpu_custom_call" | custom-call | flops 2147483648 | bytes 12582912 | tf_op jit(solution)/shard_map/kterms/pallas_call | solution.py:337
  118.2 5.1 %all-to-all-done.2 = bf16[8,256,128]{2,1,0:T(8,128)(2,1)S(1)} async-done(((bf16[8,256,128]{2,1,0:T(8,128)(2,1)}), bf16[8,256,128]{2,1,0:T(8,128)(2,1)S(1)}, u32[]{:S(2)}, u32[]{:S(2)}) %all-to-all-start.2) | async-done | bytes 524320 | tf_op jit(solution)/shard_map/all_to_all | solution.py:412
  123.2 6.1 %all-to-all-start.3 = ((bf16[64,32,128]{2,1,0:T(8,128)(2,1)}), bf16[64,32,128]{2,1,0:T(8,128)(2,1)S(1)}, u32[]{:S(2)}, u32[]{:S(2)}) async-start(bf16[64,32,128]{2,1,0:T(8,128)(2,1)} %bitcast.21), calls=%async_computation.3 | async-start | bytes 1048576 | tf_op jit(solution)/shard_map/all_to_all | solution.py:415
  129.3 1.0 convert.1
  130.4 11.7 %all-to-all-done.3 = bf16[64,32,128]{2,1,0:T(8,128)(2,1)S(1)} async-done(((bf16[64,32,128]{2,1,0:T(8,128)(2,1)}), bf16[64,32,128]{2,1,0:T(8,128)(2,1)S(1)}, u32[]{:S(2)}, u32[]{:S(2)}) %all-to-all-start.3) | async-done | bytes 524320 | tf_op jit(solution)/shard_map/all_to_all | solution.py:415
  142.1 0.7 convert_reduce_fusion
  (45 shorter events, 0.5 us)
Async XLA Ops:
  0.6 7.4 %copy-start.8 = (bf16[256,8]{0,1:T(8,128)(2,1)S(1)}, bf16[256,8]{0,1:T(8,128)(2,1)}, u32[]{:S(2)}) copy-start(bf16[256,8]{0,1:T(8,128)(2,1)} %param.13) | copy-start | bytes 12292
  0.6 7.6 %copy-start.7 = (bf16[256,8,128]{2,1,0:T(8,128)(2,1)S(1)}, bf16[256,8,128]{2,1,0:T(8,128)(2,1)}, u32[]{:S(2)}) copy-start(bf16[256,8,128]{2,1,0:T(8,128)(2,1)} %param.11) | copy-start | bytes 1572868
  1.9 6.5 %copy-start.9 = (f32[256]{0:T(256)S(1)}, f32[256]{0:T(256)}, u32[]{:S(2)}) copy-start(f32[256]{0:T(256)} %param.14) | copy-start | bytes 3076
  1.9 7.3 %copy-start.5 = (f32[256,16]{0,1:T(8,128)S(1)}, f32[256,16]{0,1:T(8,128)}, u32[]{:S(2)}) copy-start(f32[256,16]{0,1:T(8,128)} %param.10) | copy-start | bytes 49156
  1.9 7.3 %copy-start.6 = (s32[16]{0:T(128)S(1)}, s32[16]{0:T(128)}, u32[]{:S(2)}) copy-start(s32[16]{0:T(128)} %table.9) | copy-start | bytes 196
  2.8 6.4 %collective-permute-start.3 = (bf16[256,704]{1,0:T(8,128)(2,1)S(1)}, bf16[256,704]{1,0:T(8,128)(2,1)S(1)}, u32[]{:S(2)}, u32[]{:S(2)}) collective-permute-start(bf16[256,704]{1,0:T(8,128)(2,1)S(1)} %pad_maximum_fusion.refs_0_), channel_id=1, source_target_pairs={{0,8},{8,0},{1,9},{9,1},{2,10},{10,2},{3,11},{11,3},{4,12},{12,4},... | collective-permute-start | bytes 1081352 | tf_op jit(solution)/shard_map/ppermute | solution.py:356
  2.9 14.1 %collective-permute-start.2 = (bf16[256,704]{1,0:T(8,128)(2,1)S(1)}, bf16[256,704]{1,0:T(8,128)(2,1)S(1)}, u32[]{:S(2)}, u32[]{:S(2)}) collective-permute-start(bf16[256,704]{1,0:T(8,128)(2,1)S(1)} %pad_maximum_fusion.refs_0_), channel_id=1, source_target_pairs={{0,48},{16,0},{32,16},{48,32},{1,49},{17,1},{33,17},{49,33},{2,50}... | collective-permute-start | bytes 1081352 | tf_op jit(solution)/shard_map/ppermute | solution.py:356
  6.1 12.4 %collective-permute-start.1 = (bf16[256,704]{1,0:T(8,128)(2,1)S(1)}, bf16[256,704]{1,0:T(8,128)(2,1)S(1)}, u32[]{:S(2)}, u32[]{:S(2)}) collective-permute-start(bf16[256,704]{1,0:T(8,128)(2,1)S(1)} %pad_maximum_fusion.refs_0_), channel_id=1, source_target_pairs={{0,16},{16,32},{32,48},{48,0},{1,17},{17,33},{33,49},{49,1},{2,18}... | collective-permute-start | bytes 1081352 | tf_op jit(solution)/shard_map/ppermute | solution.py:356
  6.1 12.4 %collective-permute-start = (bf16[256,704]{1,0:T(8,128)(2,1)S(1)}, bf16[256,704]{1,0:T(8,128)(2,1)S(1)}, u32[]{:S(2)}, u32[]{:S(2)}) collective-permute-start(bf16[256,704]{1,0:T(8,128)(2,1)S(1)} %pad_maximum_fusion.refs_0_), channel_id=1, source_target_pairs={{0,64},{64,0},{1,65},{65,1},{2,66},{66,2},{3,67},{67,3},{4,68},{68... | collective-permute-start | bytes 1081352 | tf_op jit(solution)/shard_map/ppermute | solution.py:356
  8.5 56.6 %copy-start.1 = (s32[17]{0:T(128)}, s32[17]{0:T(128)S(1)}, u32[]{:S(2)}) copy-start(s32[17]{0:T(128)S(1)} %stack.71.ids) | copy-start | bytes 208
  9.2 2.3 %copy-start.3 = (bf16[256,16,576]{0,2,1:T(8,128)(2,1)S(1)}, bf16[256,16,576]{0,2,1:T(8,128)(2,1)}, u32[]{:S(2)}) copy-start(bf16[256,16,576]{0,2,1:T(8,128)(2,1)} %param.8) | copy-start | bytes 14155780
  18.5 3.8 %collective-permute-start.8 = (bf16[256,704]{1,0:T(8,128)(2,1)S(1)}, bf16[256,704]{1,0:T(8,128)(2,1)S(1)}, u32[]{:S(2)}, u32[]{:S(2)}) collective-permute-start(bf16[256,704]{1,0:T(8,128)(2,1)S(1)} %collective-permute-done.2.refs_2_), channel_id=1, source_target_pairs={{0,8},{8,0},{1,9},{9,1},{2,10},{10,2},{3,11},{11,3},{4,12},{12,4},... | collective-permute-start | bytes 1081352 | tf_op jit(solution)/shard_map/ppermute | solution.py:356
  18.5 3.8 %collective-permute-start.7 = (bf16[256,704]{1,0:T(8,128)(2,1)S(1)}, bf16[256,704]{1,0:T(8,128)(2,1)S(1)}, u32[]{:S(2)}, u32[]{:S(2)}) collective-permute-start(bf16[256,704]{1,0:T(8,128)(2,1)S(1)} %collective-permute-done.1.refs_1_), channel_id=1, source_target_pairs={{0,8},{8,0},{1,9},{9,1},{2,10},{10,2},{3,11},{11,3},{4,12},{12,4},... | collective-permute-start | bytes 1081352 | tf_op jit(solution)/shard_map/ppermute | solution.py:356
  19.0 3.3 %collective-permute-start.6 = (bf16[256,704]{1,0:T(8,128)(2,1)S(1)}, bf16[256,704]{1,0:T(8,128)(2,1)S(1)}, u32[]{:S(2)}, u32[]{:S(2)}) collective-permute-start(bf16[256,704]{1,0:T(8,128)(2,1)S(1)} %collective-permute-done.refs_0_), channel_id=1, source_target_pairs={{0,8},{8,0},{1,9},{9,1},{2,10},{10,2},{3,11},{11,3},{4,12},{12,4},... | collective-permute-start | bytes 1081352 | tf_op jit(solution)/shard_map/ppermute | solution.py:356
  19.0 21.2 %collective-permute-start.9 = (bf16[256,704]{1,0:T(8,128)(2,1)S(1)}, bf16[256,704]{1,0:T(8,128)(2,1)S(1)}, u32[]{:S(2)}, u32[]{:S(2)}) collective-permute-start(bf16[256,704]{1,0:T(8,128)(2,1)S(1)} %collective-permute-done.1.refs_1_), channel_id=1, source_target_pairs={{0,16},{16,32},{32,48},{48,0},{1,17},{17,33},{33,49},{49,1},{2,18}... | collective-permute-start | bytes 1081352 | tf_op jit(solution)/shard_map/ppermute | solution.py:356
  19.0 16.2 %collective-permute-start.5 = (bf16[256,704]{1,0:T(8,128)(2,1)S(1)}, bf16[256,704]{1,0:T(8,128)(2,1)S(1)}, u32[]{:S(2)}, u32[]{:S(2)}) collective-permute-start(bf16[256,704]{1,0:T(8,128)(2,1)S(1)} %collective-permute-done.refs_0_), channel_id=1, source_target_pairs={{0,48},{16,0},{32,16},{48,32},{1,49},{17,1},{33,17},{49,33},{2,50}... | collective-permute-start | bytes 1081352 | tf_op jit(solution)/shard_map/ppermute | solution.py:356
  22.2 17.9 %collective-permute-start.4 = (bf16[256,704]{1,0:T(8,128)(2,1)S(1)}, bf16[256,704]{1,0:T(8,128)(2,1)S(1)}, u32[]{:S(2)}, u32[]{:S(2)}) collective-permute-start(bf16[256,704]{1,0:T(8,128)(2,1)S(1)} %collective-permute-done.refs_0_), channel_id=1, source_target_pairs={{0,16},{16,32},{32,48},{48,0},{1,17},{17,33},{33,49},{49,1},{2,18}... | collective-permute-start | bytes 1081352 | tf_op jit(solution)/shard_map/ppermute | solution.py:356
  40.1 8.7 %collective-permute-start.10 = (bf16[256,704]{1,0:T(8,128)(2,1)S(1)}, bf16[256,704]{1,0:T(8,128)(2,1)S(1)}, u32[]{:S(2)}, u32[]{:S(2)}) collective-permute-start(bf16[256,704]{1,0:T(8,128)(2,1)S(1)} %collective-permute-done.4.refs_0_), channel_id=1, source_target_pairs={{0,8},{8,0},{1,9},{9,1},{2,10},{10,2},{3,11},{11,3},{4,12},{12,4},... | collective-permute-start | bytes 1081352 | tf_op jit(solution)/shard_map/ppermute | solution.py:356
  40.1 10.2 %collective-permute-start.12 = (bf16[256,704]{1,0:T(8,128)(2,1)S(1)}, bf16[256,704]{1,0:T(8,128)(2,1)S(1)}, u32[]{:S(2)}, u32[]{:S(2)}) collective-permute-start(bf16[256,704]{1,0:T(8,128)(2,1)S(1)} %collective-permute-done.9.refs_2_), channel_id=1, source_target_pairs={{0,8},{8,0},{1,9},{9,1},{2,10},{10,2},{3,11},{11,3},{4,12},{12,4},... | collective-permute-start | bytes 1081352 | tf_op jit(solution)/shard_map/ppermute | solution.py:356
  40.7 9.7 %collective-permute-start.11 = (bf16[256,704]{1,0:T(8,128)(2,1)S(1)}, bf16[256,704]{1,0:T(8,128)(2,1)S(1)}, u32[]{:S(2)}, u32[]{:S(2)}) collective-permute-start(bf16[256,704]{1,0:T(8,128)(2,1)S(1)} %collective-permute-done.5.refs_1_), channel_id=1, source_target_pairs={{0,8},{8,0},{1,9},{9,1},{2,10},{10,2},{3,11},{11,3},{4,12},{12,4},... | collective-permute-start | bytes 1081352 | tf_op jit(solution)/shard_map/ppermute | solution.py:356
  40.7 33.1 %all-to-all-start = ((bf16[8,784,128]{2,1,0:T(8,128)(2,1)}), bf16[8,784,128]{2,1,0:T(8,128)(2,1)}, u32[]{:S(2)}, u32[]{:S(2)}) async-start(bf16[8,784,128]{2,1,0:T(8,128)(2,1)} %get-tuple-element.44), calls=%async_computation | async-start | bytes 3211264 | tf_op jit(solution)/shard_map/all_to_all | solution.py:402
  48.3 16.8 %collective-permute-start.13 = (bf16[256,704]{1,0:T(8,128)(2,1)S(1)}, bf16[256,704]{1,0:T(8,128)(2,1)S(1)}, u32[]{:S(2)}, u32[]{:S(2)}) collective-permute-start(bf16[256,704]{1,0:T(8,128)(2,1)S(1)} %collective-permute-done.5.refs_1_), channel_id=1, source_target_pairs={{0,48},{16,0},{32,16},{48,32},{1,49},{17,1},{33,17},{49,33},{2,50}... | collective-permute-start | bytes 1081352 | tf_op jit(solution)/shard_map/ppermute | solution.py:356
  48.8 16.3 %collective-permute-start.14 = (bf16[256,704]{1,0:T(8,128)(2,1)S(1)}, bf16[256,704]{1,0:T(8,128)(2,1)S(1)}, u32[]{:S(2)}, u32[]{:S(2)}) collective-permute-start(bf16[256,704]{1,0:T(8,128)(2,1)S(1)} %collective-permute-done.10.refs_3_), channel_id=1, source_target_pairs={{0,16},{16,32},{32,48},{48,0},{1,17},{17,33},{33,49},{49,1},{2,18}... | collective-permute-start | bytes 1081352 | tf_op jit(solution)/shard_map/ppermute | solution.py:356
  50.3 2.3 %copy-start.4 = (bf16[256,16,576]{0,2,1:T(8,128)(2,1)S(1)}, bf16[256,16,576]{0,2,1:T(8,128)(2,1)}, u32[]{:S(2)}) copy-start(bf16[256,16,576]{0,2,1:T(8,128)(2,1)} %param.8) | copy-start | bytes 14155780
  73.8 19.7 %all-to-all-start.1 = ((bf16[8,512,128]{2,1,0:T(8,128)(2,1)}), bf16[8,512,128]{2,1,0:T(8,128)(2,1)S(1)}, u32[]{:S(2)}, u32[]{:S(2)}) async-start(bf16[8,512,128]{2,1,0:T(8,128)(2,1)} %get-tuple-element.55), calls=%async_computation.1 | async-start | bytes 2097152 | tf_op jit(solution)/shard_map/all_to_all | solution.py:405
  78.1 15.4 %copy-start = (f32[32,128]{1,0:T(8,128)S(1)}, f32[32,128]{1,0:T(8,128)}, u32[]{:S(2)}) copy-start(f32[32,128]{1,0:T(8,128)} %broadcast_in_dim.2.loss_ref) | copy-start | bytes 49156
  78.1 15.4 %copy-start.2 = (s32[17]{0:T(128)S(1)}, s32[17]{0:T(128)}, u32[]{:S(2)}) copy-start(s32[17]{0:T(128)} %copy-done.1) | copy-start | bytes 208
  106.8 5.2 %collective-permute-start.15 = (f32[2048,128]{1,0:T(8,128)S(1)}, f32[2048,128]{1,0:T(8,128)S(1)}, u32[]{:S(2)}, u32[]{:S(2)}) collective-permute-start(f32[2048,128]{1,0:T(8,128)S(1)} %get-tuple-element.59), channel_id=1, source_target_pairs={{0,8},{8,0},{1,9},{9,1},{2,10},{10,2},{3,11},{11,3},{4,12},{12,4},... | collective-permute-start | bytes 3145736 | tf_op jit(solution)/shard_map/ppermute | solution.py:356
  106.8 16.4 %all-to-all-start.2 = ((bf16[8,256,128]{2,1,0:T(8,128)(2,1)}), bf16[8,256,128]{2,1,0:T(8,128)(2,1)S(1)}, u32[]{:S(2)}, u32[]{:S(2)}) async-start(bf16[8,256,128]{2,1,0:T(8,128)(2,1)} %get-tuple-element.56), calls=%async_computation.2 | async-start | bytes 1048576 | tf_op jit(solution)/shard_map/all_to_all | solution.py:412
  123.2 18.9 %all-to-all-start.3 = ((bf16[64,32,128]{2,1,0:T(8,128)(2,1)}), bf16[64,32,128]{2,1,0:T(8,128)(2,1)S(1)}, u32[]{:S(2)}, u32[]{:S(2)}) async-start(bf16[64,32,128]{2,1,0:T(8,128)(2,1)} %bitcast.21), calls=%async_computation.3 | async-start | bytes 1048576 | tf_op jit(solution)/shard_map/all_to_all | solution.py:415
